TPU v7x, 128 devices: a whole 4x4x4 slice. The times are simulated.
128 devices in a mesh: shot: 8 (over x_lo, y), apert: 16 (over z, x_hi, core).
Axes of the slice: x: 4 (x_hi: 2, x_lo: 2; x = x_hi * 2 + x_lo), y: 4, z: 4, core: 2. Of those that a mesh axis runs over, the one named last changes fastest.
Arguments:
- forward_prev: float32 [8, 128, 160, 256], P('shot', 'apert'), may hold values from -0.5 to 2.5
- forward_now: float32 [8, 128, 160, 256], P('shot', 'apert'), may hold values from -0.5 to 2.5
- adjoint_prev: float32 [8, 128, 160, 256], P('shot', 'apert'), may hold values from -0.5 to 2.5
- adjoint_now: float32 [8, 128, 160, 256], P('shot', 'apert'), may hold values from -0.5 to 2.5
- velocity: bfloat16 [128, 512, 256], P('apert', 'shot'), may hold values from 0.19921875 to 0.41992188
- density: bfloat16 [128, 512, 256], P('apert', 'shot'), may hold values from 1 to 2.5
- anchors: int32 [8], P('shot'), may hold values from 0 to 352
- shot_cell: int32 [8], P('shot'), may hold values from 0 to 5242879
- wavelet: float32 [8, 6], P('shot'), may hold values from -24 to 24
- records: float32 [8, 6, 128, 160], P('shot', None, 'apert'), may hold values from -6 to 6
Outputs:
- image: float32 [128, 512, 256], P('apert', 'shot')
- adjoint_state: float32 [8, 128, 160, 256], P('shot', 'apert')
All inputs are finite; a program needn't handle non-finite values.
Results may differ from a plain program's by a relative error of at most 0.0004.
Values may be sent and summed in bfloat16 or wider, within the bound.
No kernel may reach another device: no remote copies, remote signals or barrier semaphores. Data moves between devices by JAX's collectives and lax.ppermute only.
A program may use at most 256 MiB of HBM per device.

v0:
```python
import jax
import jax.numpy as jnp
from jax import lax
from jax.sharding import PartitionSpec as P

STEPS = 6
SURF = 8


LAPLACE_WEIGHTS = (-205.0 / 72.0, 8.0 / 5.0, -1.0 / 5.0, 8.0 / 315.0, -1.0 / 560.0)
SLOPE_WEIGHTS = (4.0 / 5.0, -1.0 / 5.0, 4.0 / 105.0, -1.0 / 280.0)


def extended_2(block, sides, width):
    for axis, dim in sides:
        count = lax.axis_size(axis)
        forward = [(i, i + 1) for i in range(count - 1)]
        backward = [(target, source) for source, target in forward]
        low = lax.ppermute(
            lax.slice_in_dim(block, block.shape[dim] - width, None, axis=dim), axis, forward
        )
        high = lax.ppermute(lax.slice_in_dim(block, 0, width, axis=dim), axis, backward)
        block = jnp.concatenate([low, block, high], axis=dim)
    return block


def neighbours(extended, row_count):
    center = extended[4 : 4 + row_count]
    widths = center.shape
    padded = jnp.pad(center, ((0, 0), (4, 4), (4, 4)))
    laplacian = 3.0 * LAPLACE_WEIGHTS[0] * center
    slope_rows = jnp.zeros_like(center)
    slope_cols = jnp.zeros_like(center)
    slope_depth = jnp.zeros_like(center)
    for offset in range(1, 5):
        east_side = extended[4 + offset : 4 + offset + row_count]
        west_side = extended[4 - offset : 4 - offset + row_count]
        north_side = padded[:, 4 + offset : 4 + offset + widths[1], 4 : 4 + widths[2]]
        south_side = padded[:, 4 - offset : 4 - offset + widths[1], 4 : 4 + widths[2]]
        upper_side = padded[:, 4 : 4 + widths[1], 4 + offset : 4 + offset + widths[2]]
        lower_side = padded[:, 4 : 4 + widths[1], 4 - offset : 4 - offset + widths[2]]
        laplacian = laplacian + LAPLACE_WEIGHTS[offset] * (
            east_side + west_side + (north_side + south_side) + (upper_side + lower_side)
        )
        slope_rows = slope_rows + SLOPE_WEIGHTS[offset - 1] * (east_side - west_side)
        slope_cols = slope_cols + SLOPE_WEIGHTS[offset - 1] * (north_side - south_side)
        slope_depth = slope_depth + SLOPE_WEIGHTS[offset - 1] * (upper_side - lower_side)
    return (center, laplacian, slope_rows, slope_cols, slope_depth)


def advance(previous, extended, coefficient, slopes):
    center, laplacian, slope_rows, slope_cols, slope_depth = neighbours(extended, previous.shape[0])
    drift = slopes[0] * slope_rows + slopes[1] * slope_cols + slopes[2] * slope_depth
    return 2.0 * center - previous + coefficient * (laplacian - drift)


def place_source(field, row_start, source_cell, amount):
    height, breadth, depth = field.shape
    source_row = source_cell // (breadth * depth)
    source_col = source_cell // depth % breadth
    source_depth = source_cell % depth
    rows_here = row_start + lax.broadcasted_iota(jnp.int32, (height, 1, 1), 0)
    cols_here = lax.broadcasted_iota(jnp.int32, (1, breadth, 1), 1)
    depth_here = lax.broadcasted_iota(jnp.int32, (1, 1, depth), 2)
    struck = (rows_here == source_row) & (cols_here == source_col) & (depth_here == source_depth)
    return field + jnp.where(struck, amount, 0.0)


def tile_blocks(partial_value, begin, tile_width, owners):
    breadth = partial_value.shape[1]
    padded = jnp.pad(partial_value, ((0, 0), (tile_width, tile_width), (0, 0)))
    blocks = []
    for owner in range(owners):
        tile_start = owner * tile_width
        offset = tile_start - begin
        clipped = jnp.clip(offset, -tile_width, breadth)
        piece = lax.dynamic_slice_in_dim(padded, clipped + tile_width, tile_width, 1)
        blocks.append(piece)
    return jnp.stack(blocks)


def shards(
    forward_prev,
    forward_now,
    adjoint_prev,
    adjoint_now,
    velocity,
    density,
    anchors,
    shot_cell,
    wavelet,
    records,
):
    speed_panel, density_panel = (
        lax.all_gather(velocity, "shot", axis=1, tiled=True),
        lax.all_gather(density, "shot", axis=1, tiled=True),
    )
    row_count = forward_prev.shape[1]
    breadth = forward_prev.shape[2]
    depth = forward_prev.shape[3]
    begin = anchors[0]
    window_speed = lax.dynamic_slice_in_dim(speed_panel, begin, breadth, 1).astype(jnp.float32)
    coefficient = window_speed * window_speed
    logdens = jnp.log(
        lax.dynamic_slice_in_dim(density_panel, begin, breadth, 1).astype(jnp.float32)
    )
    log_extended = extended_2(logdens, (("apert", 0),), 4)
    unused_center, unused_lap, slope_rows, slope_cols, slope_depth = neighbours(
        log_extended, row_count
    )
    slopes = jnp.stack([slope_rows, slope_cols, slope_depth])
    first_row = lax.axis_index("apert") * row_count
    source_cell = shot_cell[0]
    record_rows = records[0]

    def propagate(previous, current, add_source):
        states = []
        for moment in range(STEPS):
            extended = extended_2(current, (("apert", 0),), 4)
            following = add_source(
                advance(previous, extended, coefficient, slopes), 0, moment, record_rows
            )
            states.append(following)
            previous, current = (current, following)
        return states

    def forward_source(field, shift, moment, unused_rows):
        return place_source(field, first_row - shift, source_cell, wavelet[0, moment])

    def receiver_source(field, moment, rows_table):
        plane = rows_table[moment]
        return field.at[:, :, SURF].add(plane)

    snapshots = propagate(forward_prev[0], forward_now[0], forward_source)
    receiver_states = propagate(
        adjoint_prev[0],
        adjoint_now[0],
        lambda field, shift, moment, unused_rows: receiver_source(field, moment, record_rows),
    )
    partial_value = jnp.zeros((row_count, breadth, depth), jnp.float32)
    for moment in range(STEPS):
        partial_value = partial_value + receiver_states[moment] * snapshots[STEPS - 1 - moment]
    tile_width = velocity.shape[1]
    owners = lax.axis_size("shot")
    blocks = tile_blocks(partial_value, begin, tile_width, owners)
    arrived = lax.all_to_all(blocks, "shot", split_axis=0, concat_axis=0, tiled=True)
    image = jnp.sum(arrived, axis=0)
    return (image, receiver_states[STEPS - 1][None])


def solution(mesh):
    placed = (
        P("shot", "apert", None, None),
        P("shot", "apert", None, None),
        P("shot", "apert", None, None),
        P("shot", "apert", None, None),
        P("apert", "shot", None),
        P("apert", "shot", None),
        P("shot"),
        P("shot"),
        P("shot", None),
        P("shot", None, "apert", None),
    )
    return jax.shard_map(
        shards,
        mesh=mesh,
        in_specs=placed,
        out_specs=(P("apert", "shot", None), P("shot", "apert", None, None)),
        check_vma=False,
    )
```

profile of v0, /device:TPU:7, one launch (start us, length us, event | category | flops | bytes accessed | tf_op | source)
XLA Modules:
  0.0 885.4 jit_solution(14718265841486082919)
XLA Ops:
  23.3 6.0 collective-permute-start.1
  38.8 24.9 %all-gather.5.cloned.1.call-done = bf16[8,512,256]{2,0,1:T(8,128)(2,1)} async-done(((bf16[8,64,256]{2,0,1:T(8,128)(2,1)}), bf16[8,512,256]{2,0,1:T(8,128)(2,1)}) %all-gather.5.cloned.1.call-update) | async-done | bytes 2097168 | tf_op jit(solution)/shard_map/all_gather | solution.py:96
  89.2 21.8 %all-gather.3.cloned.1.call-done = bf16[8,512,256]{2,0,1:T(8,128)(2,1)} async-done(((bf16[8,64,256]{2,0,1:T(8,128)(2,1)}), bf16[8,512,256]{2,0,1:T(8,128)(2,1)}) %all-gather.3.cloned.1.call-update) | async-done | bytes 2097168 | tf_op jit(solution)/shard_map/all_gather | solution.py:95
  117.1 65.9 %fusion = (f32[8,160,256]{1,0,2:T(8,128)}, f32[8,160,256]{1,0,2:T(8,128)S(1)}, f32[8,160,256]{1,0,2:T(8,128)}, f32[8,160,256]{1,0,2:T(8,128)}) fusion(f32[1,8,160,256]{2,1,3,0:T(8,128)} %copy.370, f32[4,160,256]{1,0,2:T(4,128)} %copy.371, f32[8,160,256]{1,0,2:T(8,128)} %bitcast.78, f32[4,160,256]{1,0,2:T(4,128)} %copy.372, ...), kind=kLoop, calls=%fused_computation.170 | loop fusion | flops 41287680 | bytes 12453380 | tf_op jit(solution)/shard_map/add | solution.py:66
  183.0 34.6 %fusion.102 = f32[8,160,256]{1,0,2:T(8,128)S(1)} fusion(f32[1,8,160,256]{2,1,3,0:T(8,128)} %copy.358, f32[8,160,256]{1,0,2:T(8,128)} %get-tuple-element.85, f32[8,160,256]{1,0,2:T(8,128)} %get-tuple-element.84, f32[8,160,256]{1,0,2:T(8,128)S(1)} %get-tuple-element.83, f32[4,160,256]{1,0,2:T(4,128)} %copy.361, f32[8,160,256]{1,0,2:T(8,128)} %bitcast.77, ...), kind=kLoop, calls=%fused_computation.300 | loop fusion | flops 26869760 | bytes 9830400 | tf_op jit(solution)/shard_map/add | solution.py:54
  243.3 6.0 collective-permute-start.7
  254.2 35.6 %multiply_add_fusion.4 = f32[8,160,256]{1,0,2:T(8,128)S(1)} fusion(f32[8,160,256]{1,0,2:T(8,128)} %get-tuple-element.85, f32[8,160,256]{1,0,2:T(8,128)} %get-tuple-element.84, f32[8,160,256]{1,0,2:T(8,128)S(1)} %get-tuple-element.83, f32[4,160,256]{1,0,2:T(4,128)} %copy.394, f32[8,160,256]{1,0,2:T(8,128)} %copy-done, f32[4,160,256]{1,0,2:T(4,128)} %copy.396, ...), kind=kLoop, calls=%fused_computation.349 | loop fusion | flops 26869760 | bytes 9830400 | tf_op jit(solution)/shard_map/add | solution.py:54
  298.5 6.0 collective-permute-start.19
  309.4 36.0 %fusion.1 = f32[8,160,256]{1,0,2:T(8,128)S(1)} fusion(f32[8,160,256]{1,0,2:T(8,128)} %get-tuple-element.85, f32[8,160,256]{1,0,2:T(8,128)} %get-tuple-element.84, f32[8,160,256]{1,0,2:T(8,128)S(1)} %get-tuple-element.83, f32[4,160,256]{1,0,2:T(4,128)} %copy.374, f32[8,160,256]{1,0,2:T(8,128)} %get-tuple-element.82, f32[4,160,256]{1,0,2:T(4,128)} %copy.376, ...), kind=kLoop, calls=%fused_computation.171 | loop fusion | flops 27852800 | bytes 9831940 | tf_op jit(solution)/shard_map/add | solution.py:66
  354.2 6.4 collective-permute-start.9
  365.5 34.8 %multiply_add_fusion.3 = f32[8,160,256]{1,0,2:T(8,128)S(1)} fusion(f32[8,160,256]{1,0,2:T(8,128)} %get-tuple-element.85, f32[8,160,256]{1,0,2:T(8,128)} %get-tuple-element.84, f32[8,160,256]{1,0,2:T(8,128)S(1)} %get-tuple-element.83, f32[4,160,256]{1,0,2:T(4,128)} %copy.398, f32[8,160,256]{1,0,2:T(8,128)} %copy-done.1, f32[4,160,256]{1,0,2:T(4,128)} %copy.400, ...), kind=kLoop, calls=%fused_computation.337 | loop fusion | flops 26869760 | bytes 9830400 | tf_op jit(solution)/shard_map/add | solution.py:54
  409.1 6.0 collective-permute-start.21
  419.9 35.9 %fusion.2 = f32[8,160,256]{1,0,2:T(8,128)S(1)} fusion(f32[8,160,256]{1,0,2:T(8,128)} %get-tuple-element.85, f32[8,160,256]{1,0,2:T(8,128)} %get-tuple-element.84, f32[8,160,256]{1,0,2:T(8,128)S(1)} %get-tuple-element.83, f32[4,160,256]{1,0,2:T(4,128)} %copy.378, f32[8,160,256]{1,0,2:T(8,128)} %copy-done.4, f32[4,160,256]{1,0,2:T(4,128)} %copy.380, ...), kind=kLoop, calls=%fused_computation.172 | loop fusion | flops 27852800 | bytes 9831940 | tf_op jit(solution)/shard_map/add | solution.py:66
  464.5 6.2 collective-permute-start.11
  475.5 36.4 %multiply_add_fusion.2 = f32[8,160,256]{1,0,2:T(8,128)S(1)} fusion(f32[8,160,256]{1,0,2:T(8,128)} %get-tuple-element.85, f32[8,160,256]{1,0,2:T(8,128)} %get-tuple-element.84, f32[8,160,256]{1,0,2:T(8,128)S(1)} %get-tuple-element.83, f32[4,160,256]{1,0,2:T(4,128)} %copy.402, f32[8,160,256]{1,0,2:T(8,128)} %copy-done.2, f32[4,160,256]{1,0,2:T(4,128)} %copy.404, ...), kind=kLoop, calls=%fused_computation.325 | loop fusion | flops 26869760 | bytes 9830400 | tf_op jit(solution)/shard_map/add | solution.py:54
  531.5 37.6 %fusion.3 = f32[8,160,256]{1,0,2:T(8,128)S(1)} fusion(f32[8,160,256]{1,0,2:T(8,128)} %get-tuple-element.85, f32[8,160,256]{1,0,2:T(8,128)} %get-tuple-element.84, f32[8,160,256]{1,0,2:T(8,128)S(1)} %get-tuple-element.83, f32[4,160,256]{1,0,2:T(4,128)} %copy.382, f32[8,160,256]{1,0,2:T(8,128)} %copy-done.5, f32[4,160,256]{1,0,2:T(4,128)} %copy.384, ...), kind=kLoop, calls=%fused_computation.173 | loop fusion | flops 27852800 | bytes 9831940 | tf_op jit(solution)/shard_map/add | solution.py:66
  577.9 6.2 collective-permute-start.13
  588.9 35.5 %multiply_add_fusion.1 = f32[8,160,256]{1,0,2:T(8,128)S(1)} fusion(f32[8,160,256]{1,0,2:T(8,128)} %get-tuple-element.85, f32[8,160,256]{1,0,2:T(8,128)} %get-tuple-element.84, f32[8,160,256]{1,0,2:T(8,128)S(1)} %get-tuple-element.83, f32[4,160,256]{1,0,2:T(4,128)} %copy.406, f32[8,160,256]{1,0,2:T(8,128)} %copy-done.3, f32[4,160,256]{1,0,2:T(4,128)} %copy.408, ...), kind=kLoop, calls=%fused_computation.313 | loop fusion | flops 26869760 | bytes 9830400 | tf_op jit(solution)/shard_map/add | solution.py:54
  644.1 37.6 %fusion.4 = f32[8,160,256]{1,0,2:T(8,128)S(1)} fusion(f32[8,160,256]{1,0,2:T(8,128)} %get-tuple-element.85, f32[8,160,256]{1,0,2:T(8,128)} %get-tuple-element.84, f32[8,160,256]{1,0,2:T(8,128)S(1)} %get-tuple-element.83, f32[4,160,256]{1,0,2:T(4,128)} %copy.386, f32[8,160,256]{1,0,2:T(8,128)} %copy-done.7, f32[4,160,256]{1,0,2:T(4,128)} %copy.388, ...), kind=kLoop, calls=%fused_computation.174 | loop fusion | flops 27852800 | bytes 9831940 | tf_op jit(solution)/shard_map/add | solution.py:66
  701.2 35.4 %multiply_add_fusion = f32[8,160,256]{1,0,2:T(8,128)} fusion(f32[8,160,256]{1,0,2:T(8,128)} %get-tuple-element.85, f32[8,160,256]{1,0,2:T(8,128)} %get-tuple-element.84, f32[8,160,256]{1,0,2:T(8,128)S(1)} %get-tuple-element.83, f32[4,160,256]{1,0,2:T(4,128)} %copy.410, f32[8,160,256]{1,0,2:T(8,128)} %copy-done.6, f32[4,160,256]{1,0,2:T(4,128)} %copy.412, ...), kind=kLoop, calls=%fused_computation.301 | loop fusion | flops 26869760 | bytes 9830400 | tf_op jit(solution)/shard_map/add | solution.py:54
  742.8 44.0 %fusion.11 = f32[8,160,256]{1,0,2:T(8,128)} fusion(f32[8,160,256]{1,0,2:T(8,128)} %copy-done, f32[8,160,256]{1,0,2:T(8,128)} %fusion.103, f32[8,160,256]{1,0,2:T(8,128)} %get-tuple-element.82, f32[8,160,256]{1,0,2:T(8,128)} %copy-done.6, f32[8,160,256]{1,0,2:T(8,128)} %copy-done.4, f32[8,160,256]{1,0,2:T(8,128)} %copy-done.3, f32[8,160,256]{1,0,2:T(8,128)} %copy-done.5, ...), kind=kLoop, calls=%fused_computation.181 | loop fusion | flops 31457280 | bytes 21628420 | tf_op jit(solution)/shard_map/add | solution.py:142
  786.8 11.4 %pad_dynamic-slice_fusion = (f32[8,64,256]{1,0,2:T(8,128)S(1)}, f32[8,64,256]{1,0,2:T(8,128)}, f32[8,64,256]{1,0,2:T(8,128)}, f32[8,64,256]{1,0,2:T(8,128)}, f32...) fusion(s32[]{:T(128)S(6)} %select_n.113, ...), kind=kLoop, calls=%fused_computation.156 | loop fusion | bytes 5505056 | tf_op jit(solution)/shard_map/dynamic_slice | solution.py:77
  821.8 7.6 all-to-all-start
  831.1 43.7 %all-to-all-done = f32[8,8,64,256]{3,2,1,0:T(8,128)} async-done(((f32[8,8,64,256]{3,2,1,0:T(8,128)}), f32[8,8,64,256]{3,2,1,0:T(8,128)}, u32[]{:S(2)}, u32[]{:S(2)}) %all-to-all-start) | async-done | bytes 4194336 | tf_op jit(solution)/shard_map/all_to_all | solution.py:146
  (190 shorter events, 246.6 us)
Async XLA Ops:
  7.2 56.5 %all-gather.5.cloned.1.call-start = ((), (), s32[]{:S(2)}) async-start(), calls=%async_computation.2 | async-start | bytes 2359296 | tf_op jit(solution)/shard_map/all_gather | solution.py:96
  9.2 101.9 %all-gather.3.cloned.1.call-start = ((), (), s32[]{:S(2)}) async-start(), calls=%async_computation.1 | async-start | bytes 2359296 | tf_op jit(solution)/shard_map/all_gather | solution.py:95
  12.3 64.4 %collective-permute-start.4 = (f32[4,160,256]{2,1,0:T(8,128)}, f32[4,160,256]{2,1,0:T(8,128)}, u32[]{:S(2)}, u32[]{:S(2)}) collective-permute-start(f32[4,160,256]{2,1,0:T(8,128)} %get-tuple-element.119), channel_id=1, source_target_pairs={{1,0},{2,1},{3,2},{4,3},{5,4},{6,5},{7,6},{8,7},{9,8},{10,9},{11,1... | collective-permute-start | bytes 1966088 | tf_op jit(solution)/shard_map/ppermute | solution.py:22
  14.9 67.1 %collective-permute-start.5 = (f32[4,160,256]{2,1,0:T(8,128)}, f32[4,160,256]{2,1,0:T(8,128)}, u32[]{:S(2)}, u32[]{:S(2)}) collective-permute-start(f32[4,160,256]{2,1,0:T(8,128)} %get-tuple-element.118), channel_id=1, source_target_pairs={{0,1},{1,2},{2,3},{3,4},{4,5},{5,6},{6,7},{7,8},{8,9},{9,10},{10,1... | collective-permute-start | bytes 1966088 | tf_op jit(solution)/shard_map/ppermute | solution.py:19
  21.4 63.0 %collective-permute-start = (f32[4,160,256]{2,1,0:T(8,128)}, f32[4,160,256]{2,1,0:T(8,128)}, u32[]{:S(2)}, u32[]{:S(2)}) collective-permute-start(f32[4,160,256]{2,1,0:T(8,128)} %get-tuple-element.117), channel_id=1, source_target_pairs={{1,0},{2,1},{3,2},{4,3},{5,4},{6,5},{7,6},{8,7},{9,8},{10,9},{11,1... | collective-permute-start | bytes 1966088 | tf_op jit(solution)/shard_map/ppermute | solution.py:22
  23.3 63.5 %collective-permute-start.1 = (f32[4,160,256]{2,1,0:T(8,128)}, f32[4,160,256]{2,1,0:T(8,128)}, u32[]{:S(2)}, u32[]{:S(2)}) collective-permute-start(f32[4,160,256]{2,1,0:T(8,128)} %get-tuple-element.116), channel_id=1, source_target_pairs={{0,1},{1,2},{2,3},{3,4},{4,5},{5,6},{6,7},{7,8},{8,9},{9,10},{10,1... | collective-permute-start | bytes 1966088 | tf_op jit(solution)/shard_map/ppermute | solution.py:19
  238.8 65.7 %collective-permute-start.6 = (f32[4,160,256]{2,1,0:T(8,128)}, f32[4,160,256]{2,1,0:T(8,128)}, u32[]{:S(2)}, u32[]{:S(2)}) collective-permute-start(f32[4,160,256]{2,1,0:T(8,128)} %copy.373), channel_id=1, source_target_pairs={{1,0},{2,1},{3,2},{4,3},{5,4},{6,5},{7,6},{8,7},{9,8},{10,9},{11,1... | collective-permute-start | bytes 1966088 | tf_op jit(solution)/shard_map/ppermute | solution.py:22
  243.3 63.6 %collective-permute-start.7 = (f32[4,160,256]{2,1,0:T(8,128)}, f32[4,160,256]{2,1,0:T(8,128)}, u32[]{:S(2)}, u32[]{:S(2)}) collective-permute-start(f32[4,160,256]{2,1,0:T(8,128)} %copy.375), channel_id=1, source_target_pairs={{0,1},{1,2},{2,3},{3,4},{4,5},{5,6},{6,7},{7,8},{8,9},{9,10},{10,1... | collective-permute-start | bytes 1966088 | tf_op jit(solution)/shard_map/ppermute | solution.py:19
  294.2 66.5 %collective-permute-start.18 = (f32[4,160,256]{2,1,0:T(8,128)}, f32[4,160,256]{2,1,0:T(8,128)}, u32[]{:S(2)}, u32[]{:S(2)}) collective-permute-start(f32[4,160,256]{2,1,0:T(8,128)} %copy.397), channel_id=1, source_target_pairs={{1,0},{2,1},{3,2},{4,3},{5,4},{6,5},{7,6},{8,7},{9,8},{10,9},{11,1... | collective-permute-start | bytes 1966088 | tf_op jit(solution)/shard_map/ppermute | solution.py:22
  298.5 64.6 %collective-permute-start.19 = (f32[4,160,256]{2,1,0:T(8,128)}, f32[4,160,256]{2,1,0:T(8,128)}, u32[]{:S(2)}, u32[]{:S(2)}) collective-permute-start(f32[4,160,256]{2,1,0:T(8,128)} %copy.399), channel_id=1, source_target_pairs={{0,1},{1,2},{2,3},{3,4},{4,5},{5,6},{6,7},{7,8},{8,9},{9,10},{10,1... | collective-permute-start | bytes 1966088 | tf_op jit(solution)/shard_map/ppermute | solution.py:19
  349.9 65.2 %collective-permute-start.8 = (f32[4,160,256]{2,1,0:T(8,128)}, f32[4,160,256]{2,1,0:T(8,128)}, u32[]{:S(2)}, u32[]{:S(2)}) collective-permute-start(f32[4,160,256]{2,1,0:T(8,128)} %copy.377), channel_id=1, source_target_pairs={{1,0},{2,1},{3,2},{4,3},{5,4},{6,5},{7,6},{8,7},{9,8},{10,9},{11,1... | collective-permute-start | bytes 1966088 | tf_op jit(solution)/shard_map/ppermute | solution.py:22
  354.2 63.3 %collective-permute-start.9 = (f32[4,160,256]{2,1,0:T(8,128)}, f32[4,160,256]{2,1,0:T(8,128)}, u32[]{:S(2)}, u32[]{:S(2)}) collective-permute-start(f32[4,160,256]{2,1,0:T(8,128)} %copy.379), channel_id=1, source_target_pairs={{0,1},{1,2},{2,3},{3,4},{4,5},{5,6},{6,7},{7,8},{8,9},{9,10},{10,1... | collective-permute-start | bytes 1966088 | tf_op jit(solution)/shard_map/ppermute | solution.py:19
  404.8 65.9 %collective-permute-start.20 = (f32[4,160,256]{2,1,0:T(8,128)}, f32[4,160,256]{2,1,0:T(8,128)}, u32[]{:S(2)}, u32[]{:S(2)}) collective-permute-start(f32[4,160,256]{2,1,0:T(8,128)} %copy.401), channel_id=1, source_target_pairs={{1,0},{2,1},{3,2},{4,3},{5,4},{6,5},{7,6},{8,7},{9,8},{10,9},{11,1... | collective-permute-start | bytes 1966088 | tf_op jit(solution)/shard_map/ppermute | solution.py:22
  409.1 64.0 %collective-permute-start.21 = (f32[4,160,256]{2,1,0:T(8,128)}, f32[4,160,256]{2,1,0:T(8,128)}, u32[]{:S(2)}, u32[]{:S(2)}) collective-permute-start(f32[4,160,256]{2,1,0:T(8,128)} %copy.403), channel_id=1, source_target_pairs={{0,1},{1,2},{2,3},{3,4},{4,5},{5,6},{6,7},{7,8},{8,9},{9,10},{10,1... | collective-permute-start | bytes 1966088 | tf_op jit(solution)/shard_map/ppermute | solution.py:19
  460.1 66.5 %collective-permute-start.10 = (f32[4,160,256]{2,1,0:T(8,128)}, f32[4,160,256]{2,1,0:T(8,128)}, u32[]{:S(2)}, u32[]{:S(2)}) collective-permute-start(f32[4,160,256]{2,1,0:T(8,128)} %copy.381), channel_id=1, source_target_pairs={{1,0},{2,1},{3,2},{4,3},{5,4},{6,5},{7,6},{8,7},{9,8},{10,9},{11,1... | collective-permute-start | bytes 1966088 | tf_op jit(solution)/shard_map/ppermute | solution.py:22
  464.5 64.6 %collective-permute-start.11 = (f32[4,160,256]{2,1,0:T(8,128)}, f32[4,160,256]{2,1,0:T(8,128)}, u32[]{:S(2)}, u32[]{:S(2)}) collective-permute-start(f32[4,160,256]{2,1,0:T(8,128)} %copy.383), channel_id=1, source_target_pairs={{0,1},{1,2},{2,3},{3,4},{4,5},{5,6},{6,7},{7,8},{8,9},{9,10},{10,1... | collective-permute-start | bytes 1966088 | tf_op jit(solution)/shard_map/ppermute | solution.py:19
  516.3 67.8 %collective-permute-start.22 = (f32[4,160,256]{2,1,0:T(8,128)}, f32[4,160,256]{2,1,0:T(8,128)}, u32[]{:S(2)}, u32[]{:S(2)}) collective-permute-start(f32[4,160,256]{2,1,0:T(8,128)} %copy.405), channel_id=1, source_target_pairs={{1,0},{2,1},{3,2},{4,3},{5,4},{6,5},{7,6},{8,7},{9,8},{10,9},{11,1... | collective-permute-start | bytes 1966088 | tf_op jit(solution)/shard_map/ppermute | solution.py:22
  520.6 65.9 %collective-permute-start.23 = (f32[4,160,256]{2,1,0:T(8,128)}, f32[4,160,256]{2,1,0:T(8,128)}, u32[]{:S(2)}, u32[]{:S(2)}) collective-permute-start(f32[4,160,256]{2,1,0:T(8,128)} %copy.407), channel_id=1, source_target_pairs={{0,1},{1,2},{2,3},{3,4},{4,5},{5,6},{6,7},{7,8},{8,9},{9,10},{10,1... | collective-permute-start | bytes 1966088 | tf_op jit(solution)/shard_map/ppermute | solution.py:19
  573.6 65.7 %collective-permute-start.12 = (f32[4,160,256]{2,1,0:T(8,128)}, f32[4,160,256]{2,1,0:T(8,128)}, u32[]{:S(2)}, u32[]{:S(2)}) collective-permute-start(f32[4,160,256]{2,1,0:T(8,128)} %copy.385), channel_id=1, source_target_pairs={{1,0},{2,1},{3,2},{4,3},{5,4},{6,5},{7,6},{8,7},{9,8},{10,9},{11,1... | collective-permute-start | bytes 1966088 | tf_op jit(solution)/shard_map/ppermute | solution.py:22
  577.9 63.7 %collective-permute-start.13 = (f32[4,160,256]{2,1,0:T(8,128)}, f32[4,160,256]{2,1,0:T(8,128)}, u32[]{:S(2)}, u32[]{:S(2)}) collective-permute-start(f32[4,160,256]{2,1,0:T(8,128)} %copy.387), channel_id=1, source_target_pairs={{0,1},{1,2},{2,3},{3,4},{4,5},{5,6},{6,7},{7,8},{8,9},{9,10},{10,1... | collective-permute-start | bytes 1966088 | tf_op jit(solution)/shard_map/ppermute | solution.py:19
  628.9 67.6 %collective-permute-start.24 = (f32[4,160,256]{2,1,0:T(8,128)}, f32[4,160,256]{2,1,0:T(8,128)}, u32[]{:S(2)}, u32[]{:S(2)}) collective-permute-start(f32[4,160,256]{2,1,0:T(8,128)} %copy.409), channel_id=1, source_target_pairs={{1,0},{2,1},{3,2},{4,3},{5,4},{6,5},{7,6},{8,7},{9,8},{10,9},{11,1... | collective-permute-start | bytes 1966088 | tf_op jit(solution)/shard_map/ppermute | solution.py:22
  633.2 65.7 %collective-permute-start.25 = (f32[4,160,256]{2,1,0:T(8,128)}, f32[4,160,256]{2,1,0:T(8,128)}, u32[]{:S(2)}, u32[]{:S(2)}) collective-permute-start(f32[4,160,256]{2,1,0:T(8,128)} %copy.411), channel_id=1, source_target_pairs={{0,1},{1,2},{2,3},{3,4},{4,5},{5,6},{6,7},{7,8},{8,9},{9,10},{10,1... | collective-permute-start | bytes 1966088 | tf_op jit(solution)/shard_map/ppermute | solution.py:19
  686.0 50.6 %collective-permute-start.14 = (f32[4,160,256]{2,1,0:T(8,128)}, f32[4,160,256]{2,1,0:T(8,128)}, u32[]{:S(2)}, u32[]{:S(2)}) collective-permute-start(f32[4,160,256]{2,1,0:T(8,128)} %copy.389), channel_id=1, source_target_pairs={{1,0},{2,1},{3,2},{4,3},{5,4},{6,5},{7,6},{8,7},{9,8},{10,9},{11,1... | collective-permute-start | bytes 1966088 | tf_op jit(solution)/shard_map/ppermute | solution.py:22
  821.8 53.0 %all-to-all-start = ((f32[8,8,64,256]{3,2,1,0:T(8,128)}), f32[8,8,64,256]{3,2,1,0:T(8,128)}, u32[]{:S(2)}, u32[]{:S(2)}) async-start(f32[8,8,64,256]{3,2,1,0:T(8,128)} %bitcast_dynamic-update-slice_fusion), calls=%async_computation | async-start | bytes 8388608 | tf_op jit(solution)/shard_map/all_to_all | solution.py:146
  (25 other events, 293.2 us)
Sparse Core Ops, SparseCore 0:
  10.2 53.3 all-gather.4
  65.9 45.1 all-gather.2
where the time goes:
time: 892 us; the launch traced here: 885 us
  other arithmetic  474 us (53%)
  local copies, waits for them, and re-layouts  192 us (22%)
  starting transfers between devices  111 us (12%)
  waiting for transfers between devices  90.6 us (10%)
  between operations  16.8 us (2%)
    add x5, other arithmetic, place_source(): return field + jnp.where(struck, amount, 0.0)  213 us
    add x6, other arithmetic, advance(): return 2.0 * center - previous + coefficient * (laplacian - drift)  212 us
    ppermute x13, starting transfers between devices, extended_2(): lax.ppermute(lax.slice_in_dim(block, block.shape[dim] - width, None, axis...  75.4 us
    slice x23, local copies, waits for them, and re-layouts, extended_2(): lax.slice_in_dim(block, block.shape[dim] - width, None, axis=dim)  49.5 us
    add x1, other arithmetic, shards(): partial_value + receiver_states[moment] * snapshots[STEPS - 1 - moment]  44 us
    all_to_all x1, waiting for transfers between devices, shards(): lax.all_to_all(blocks, 'shot', split_axis=0, concat_axis=0, tiled=True)  43.7 us
    ppermute x13, local copies, waits for them, and re-layouts, extended_2(): lax.ppermute(lax.slice_in_dim(block, block.shape[dim] - width, None, axis...  31.5 us
    ppermute x13, local copies, waits for them, and re-layouts, extended_2(): lax.ppermute(lax.slice_in_dim(block, 0, width, axis=dim), axis, backward)  30.1 us
  transfers between devices with their start and end apart: 29, of which 3 were waited for; matrix products, arithmetic and copies ran while one was open for 53% of the time, Pallas kernels for 0%

commit v1 on v0

v1 whole, which is shorter than its diff:
```python
import functools

import jax
import jax.numpy as jnp
import ml_dtypes
import numpy as np
from jax import lax
from jax.experimental import pallas as pl
from jax.experimental.pallas import tpu as pltpu
from jax.sharding import PartitionSpec as P

STEPS = 6
SURF = 8
ROWS, COLS, DEPTH = 8, 160, 256
TILE = 64
LAP = (-14350.0, 8064.0, -1008.0, 128.0, -9.0)
SLOPE = (672.0, -168.0, 32.0, -3.0)
LAP_SCALE, SLOPE_SCALE = 1.0 / 5040.0, 1.0 / 840.0
F32, BF16 = jnp.float32, jnp.bfloat16
VMEM = pl.BlockSpec(memory_space=pltpu.VMEM)
SMEM = pl.BlockSpec(memory_space=pltpu.SMEM)
PARAMS = pltpu.CompilerParams(vmem_limit_bytes=56 * 1024 * 1024)


def banded(size):
    lap, slope = np.zeros((size, size)), np.zeros((size, size))
    for k in range(1, 5):
        lap += LAP[k] * (np.eye(size, k=k) + np.eye(size, k=-k))
        slope += SLOPE[k - 1] * (np.eye(size, k=k) - np.eye(size, k=-k))
    return lap, slope


def weight_tables():
    lap, slope = banded(DEPTH)
    depth_table = np.concatenate([lap.T, slope.T], axis=1).astype(ml_dtypes.bfloat16)
    lap, slope = banded(COLS)
    cols_table = np.concatenate([lap, slope], axis=0).astype(ml_dtypes.bfloat16)
    return jnp.asarray(depth_table), jnp.asarray(cols_table)


def halves(x):
    high = x.astype(BF16)
    return high, (x - high.astype(F32)).astype(BF16)


def in_plane(src, depth_w, cols_w, zz, cc):
    def body(r, carry):
        high, low = halves(src[4 + r])
        zz[r] = jnp.dot(high, depth_w[...], preferred_element_type=F32) + jnp.dot(
            low, depth_w[...], preferred_element_type=F32
        )
        cc[r] = jnp.dot(cols_w[...], high, preferred_element_type=F32) + jnp.dot(
            cols_w[...], low, preferred_element_type=F32
        )
        return carry

    lax.fori_loop(0, ROWS, body, 0)


def load_extended(ext, now, parity, core_rows, cross_rows):
    ext[4 : 4 + ROWS] = now[...]
    core_at = pl.multiple_of((1 - parity) * 12, 4)
    cross_at = pl.multiple_of(parity * 12, 4)
    ext[pl.ds(core_at, 4)] = core_rows
    ext[pl.ds(cross_at, 4)] = cross_rows


def slopes_kernel(info, vel, dens, core, cross, depth_w, cols_w, coef, s0, s1, s2, ext, zz, cc):
    parity, outer = info[0], info[1]
    pad = jnp.where(outer == 1, 1.0, 0.0).astype(F32)
    core_at = pl.multiple_of((1 - parity) * 12, 4)
    cross_at = pl.multiple_of(parity * 12, 4)
    ext[4 : 4 + ROWS] = jnp.log(dens[...].astype(F32))
    ext[pl.ds(core_at, 4)] = jnp.log(core[...].astype(F32))
    ext[pl.ds(cross_at, 4)] = jnp.log(cross[...].astype(F32) + pad)
    in_plane(ext, depth_w, cols_w, zz, cc)

    def body(i, carry):
        at = pl.ds(pl.multiple_of(i * 8, 8), 8)
        at2 = pl.ds(pl.multiple_of(COLS + i * 8, 8), 8)
        e = [ext[r, at, :] for r in range(16)]
        for r in range(ROWS):
            speed = vel[r, at, :]
            c = speed * speed
            d0 = SLOPE[0] * (e[r + 5] - e[r + 3])
            for k in range(2, 5):
                d0 += SLOPE[k - 1] * (e[r + 4 + k] - e[r + 4 - k])
            coef[r, at, :] = c * LAP_SCALE
            cs = c * (SLOPE_SCALE * SLOPE_SCALE)
            s0[r, at, :] = cs * d0
            s1[r, at, :] = cs * cc[r, at2, :]
            s2[r, at, :] = cs * zz[r, at, DEPTH:]
        return carry

    lax.fori_loop(0, COLS // 8, body, 0)


def step_kernel(mode, first, *refs):
    refs = list(refs)
    info = refs.pop(0)
    amount = refs.pop(0) if mode == "fwd" else None
    prev, now, core, cross = refs[:4]
    refs = refs[4:]
    if first:
        qs_now = None
    else:
        qr_now, qr_prev, qs_now, qs_prev = refs[:4]
        refs = refs[4:]
    plane = refs.pop(0) if mode == "bwd" else None
    coef, s0, s1, s2, depth_w, cols_w = refs[:6]
    refs = refs[6:]
    out = refs.pop(0)
    last = len(refs) == 3
    if not last:
        core_out, cross_out, qr_out, qs_out = refs[:4]
        refs = refs[4:]
    ext, zz, cc = refs
    parity = info[0]
    if first:
        seen = cross[...]
    else:
        seen = (2.0 * qr_now[...] - qr_prev[...]) + cross[...].astype(F32)
    load_extended(ext, now, parity, core[...], seen)
    if not last:
        qr_out[...] = seen
    in_plane(ext, depth_w, cols_w, zz, cc)

    def body(i, carry):
        at = pl.ds(pl.multiple_of(i * 8, 8), 8)
        at2 = pl.ds(pl.multiple_of(COLS + i * 8, 8), 8)
        e = [ext[r, at, :] for r in range(16)]
        for r in range(ROWS):
            mid = e[r + 4]
            lap = (3.0 * LAP[0]) * mid + (cc[r, at, :] + zz[r, at, :DEPTH])
            d0 = None
            for k in range(1, 5):
                hi, lo = e[r + 4 + k], e[r + 4 - k]
                lap += LAP[k] * (hi + lo)
                term = SLOPE[k - 1] * (hi - lo)
                d0 = term if d0 is None else d0 + term
            drift = s0[r, at, :] * d0 + s1[r, at, :] * cc[r, at2, :] + s2[r, at, :] * zz[r, at, DEPTH:]
            new = 2.0 * mid - prev[r, at, :] + (coef[r, at, :] * lap - drift)
            if mode == "bwd":
                out[r, at, :128] = new[:, :128] + plane[r, at, :]
                out[r, at, 128:] = new[:, 128:]
            else:
                out[r, at, :] = new
        return carry

    lax.fori_loop(0, COLS // 8, body, 0)

    if mode == "fwd":

        @pl.when(info[2] == 1)
        def _():
            row, col = info[3], info[4]
            base = pl.multiple_of((col // 8) * 8, 8)
            col_in = lax.broadcasted_iota(jnp.int32, (8, DEPTH), 0)
            depth_in = lax.broadcasted_iota(jnp.int32, (8, DEPTH), 1)
            struck = (col_in == col - base) & (depth_in == info[5])
            out[row, pl.ds(base, 8), :] += jnp.where(struck, amount[0], 0.0)

    if not last:
        core_out[...] = out[pl.ds(pl.multiple_of((1 - parity) * 4, 4), 4)]
        rows = out[pl.ds(pl.multiple_of(parity * 4, 4), 4)]
        if first:
            own = now[pl.ds(pl.multiple_of(parity * 4, 4), 4)]
            base = own
        else:
            base = 2.0 * qs_now[...] - qs_prev[...]
        sent = (rows - base).astype(BF16)
        cross_out[...] = sent
        qs_out[...] = base + sent.astype(F32)


def step(mode, info, amount, prev, now, core, cross, quant, plane, fields, tables, last):
    first = quant is None
    args = [info]
    specs = [SMEM]
    if mode == "fwd":
        args.append(amount)
        specs.append(SMEM)
    args += [prev, now, core, cross]
    if not first:
        args += list(quant)
    if mode == "bwd":
        args.append(plane)
    args += list(fields) + list(tables)
    specs += [VMEM] * (len(args) - len(specs))
    slab = jax.ShapeDtypeStruct((ROWS, COLS, DEPTH), F32)
    face = jax.ShapeDtypeStruct((4, COLS, DEPTH), F32)
    outs = [slab]
    if not last:
        outs += [face, jax.ShapeDtypeStruct((4, COLS, DEPTH), BF16), face, face]
    return pl.pallas_call(
        functools.partial(step_kernel, mode, first),
        out_shape=outs,
        in_specs=specs,
        out_specs=[VMEM] * len(outs),
        scratch_shapes=[
            pltpu.VMEM((ROWS + 8, COLS, DEPTH), F32),
            pltpu.VMEM((ROWS, COLS, 2 * DEPTH), F32),
            pltpu.VMEM((ROWS, 2 * COLS, DEPTH), F32),
        ],
        compiler_params=PARAMS,
        cost_estimate=pl.CostEstimate(flops=1_500_000_000, bytes_accessed=12_000_000, transcendentals=0),
        name="step_" + mode,
    )(*args)


def window_kernel(info, t0, t1, t2, t3, vel_out, dens_out, core_out, cross_out, wide, shifted):
    parity, offset = info[0], info[1]
    want = lax.broadcasted_iota(jnp.int32, (COLS, TILE), 0) + offset
    within = lax.broadcasted_iota(jnp.int32, (COLS, TILE), 1)
    pick = jnp.concatenate(
        [jnp.where(within + info[2 + s] * TILE == want, 1.0, 0.0) for s in range(4)], axis=1
    ).astype(BF16)
    for which in range(2):
        for s, tile in enumerate((t0, t1, t2, t3)):
            wide[:, s * TILE : (s + 1) * TILE, :] = tile[which]
        target = vel_out if which == 0 else shifted
        for r in range(ROWS):
            target[r] = jnp.dot(pick, wide[r], preferred_element_type=F32)
    dens_out[...] = shifted[...].astype(BF16)
    core_out[...] = shifted[pl.ds(pl.multiple_of((1 - parity) * 4, 4), 4)].astype(BF16)
    cross_out[...] = shifted[pl.ds(pl.multiple_of(parity * 4, 4), 4)].astype(BF16)


def blocks_kernel(info, part, a5, s0, a0, s5, b0, b1, b2, b3):
    within = lax.broadcasted_iota(jnp.int32, (TILE, COLS), 0)
    column = lax.broadcasted_iota(jnp.int32, (TILE, COLS), 1) + info[0]
    pick = jnp.concatenate(
        [jnp.where(within + info[1 + s] * TILE == column, 1.0, 0.0) for s in range(4)], axis=0
    ).astype(BF16)
    for r in range(ROWS):
        total = part[r] + a5[r] * s0[r] + a0[r] * s5[r]
        high, low = halves(total)
        placed = jnp.dot(pick, high, preferred_element_type=F32) + jnp.dot(
            pick, low, preferred_element_type=F32
        )
        for s, block in enumerate((b0, b1, b2, b3)):
            block[r] = placed[s * TILE : (s + 1) * TILE]


def shards(
    forward_prev,
    forward_now,
    adjoint_prev,
    adjoint_now,
    velocity,
    density,
    anchors,
    shot_cell,
    wavelet,
    records,
):
    tables = weight_tables()
    place = lax.axis_index("apert")
    shot = lax.axis_index("shot")
    count = lax.axis_size("apert")
    groups = lax.axis_size("shot")
    half = groups // 2
    parity = place & 1
    core_pairs = [(i, i ^ 1) for i in range(count)]
    cross_pairs = [(i, i + 1) for i in range(1, count - 1, 2)] + [(i + 1, i) for i in range(1, count - 1, 2)]
    side_pairs = [(i, (i + half) % groups) for i in range(groups)]

    def ring_pairs(shift):
        return [(i, (i // half) * half + (i % half + shift) % half) for i in range(groups)]

    def faces(field):
        return (
            lax.dynamic_slice_in_dim(field, (1 - parity) * 4, 4, 0),
            lax.dynamic_slice_in_dim(field, parity * 4, 4, 0),
        )

    def swap(core, cross):
        return lax.ppermute(core, "apert", core_pairs), lax.ppermute(cross, "apert", cross_pairs)

    starts = lax.all_gather(anchors[0], "shot")
    both = jnp.stack([velocity, density])
    other = lax.ppermute(both, "shot", side_pairs)
    upper = shot // half
    ring = shot % half

    def tile_of(group):
        first = starts[group] // TILE
        return (first + (ring - first) % half) // half

    tiles = []
    for shift in range(half):
        group = upper * half + (ring + shift) % half
        piece = jnp.where(tile_of(group) == upper, both, other)
        tiles.append(piece if shift == 0 else lax.ppermute(piece, "shot", ring_pairs(shift)))
    begin = anchors[0]
    first_tile = begin // TILE
    offset = begin - first_tile * TILE

    fwd_prev, fwd_now, bwd_prev, bwd_now = forward_prev[0], forward_now[0], adjoint_prev[0], adjoint_now[0]
    fwd_core, fwd_cross = swap(*faces(fwd_now))
    bwd_core, bwd_cross = swap(*faces(bwd_now))

    slots = [(ring - shift - first_tile) % half for shift in range(half)]
    info = jnp.stack([parity, offset] + slots).astype(jnp.int32)
    slab = jax.ShapeDtypeStruct((ROWS, COLS, DEPTH), F32)
    thin = jax.ShapeDtypeStruct((4, COLS, DEPTH), BF16)
    vel, dens, dens_core, dens_cross = pl.pallas_call(
        window_kernel,
        out_shape=[slab, jax.ShapeDtypeStruct((ROWS, COLS, DEPTH), BF16), thin, thin],
        in_specs=[SMEM] + [VMEM] * 4,
        out_specs=[VMEM] * 4,
        scratch_shapes=[pltpu.VMEM((ROWS, 4 * TILE, DEPTH), BF16), pltpu.VMEM((ROWS, COLS, DEPTH), F32)],
        compiler_params=PARAMS,
        name="window",
    )(info, *tiles)
    dens_core, dens_cross = swap(dens_core, dens_cross)
    outer = ((place == 0) | (place == count - 1)).astype(jnp.int32)
    info = jnp.stack([parity, outer]).astype(jnp.int32)
    fields = pl.pallas_call(
        slopes_kernel,
        out_shape=[slab] * 4,
        in_specs=[SMEM] + [VMEM] * 6,
        out_specs=[VMEM] * 4,
        scratch_shapes=[
            pltpu.VMEM((ROWS + 8, COLS, DEPTH), F32),
            pltpu.VMEM((ROWS, COLS, 2 * DEPTH), F32),
            pltpu.VMEM((ROWS, 2 * COLS, DEPTH), F32),
        ],
        compiler_params=PARAMS,
        name="slopes",
    )(info, vel, dens, dens_core, dens_cross, *tables)

    cell = shot_cell[0]
    row = cell // (COLS * DEPTH) - place * ROWS
    here = ((row >= 0) & (row < ROWS)).astype(jnp.int32)
    info = jnp.stack(
        [parity, outer, here, jnp.clip(row, 0, ROWS - 1), cell // DEPTH % COLS, cell % DEPTH]
    ).astype(jnp.int32)
    lane = lax.broadcasted_iota(jnp.int32, (1, 1, 1, 128), 3)
    planes = jnp.where(lane == SURF, records[0][..., None], 0.0)

    fwd_quant = bwd_quant = None
    snapshots, states = [], []
    part = None
    for moment in range(STEPS):
        last = moment == STEPS - 1
        if moment > 0:
            fwd_core, fwd_cross = swap(fwd_core, fwd_cross)
        new, *sent = step(
            "fwd", info, wavelet[0, moment : moment + 1], fwd_prev, fwd_now, fwd_core, fwd_cross,
            fwd_quant, None, fields, tables, last,
        )
        if not last:
            own = faces(fwd_now)[1] if moment == 0 else fwd_quant[2]
            fwd_core, fwd_cross, seen, shown = sent
            fwd_quant = (seen, seen if moment == 0 else fwd_quant[0], shown, own)
        snapshots.append(new)
        fwd_prev, fwd_now = fwd_now, new

        if moment > 0:
            bwd_core, bwd_cross = swap(bwd_core, bwd_cross)
        new, *sent = step(
            "bwd", info, None, bwd_prev, bwd_now, bwd_core, bwd_cross,
            bwd_quant, planes[moment], fields, tables, last,
        )
        if not last:
            own = faces(bwd_now)[1] if moment == 0 else bwd_quant[2]
            bwd_core, bwd_cross, seen, shown = sent
            bwd_quant = (seen, seen if moment == 0 else bwd_quant[0], shown, own)
        states.append(new)
        bwd_prev, bwd_now = bwd_now, new
    part = sum(states[t] * snapshots[STEPS - 1 - t] for t in range(1, STEPS - 1))

    slots = [(ring + shift - first_tile) % half for shift in range(half)]
    info = jnp.stack([offset] + slots).astype(jnp.int32)
    block = jax.ShapeDtypeStruct((ROWS, TILE, DEPTH), F32)
    blocks = pl.pallas_call(
        blocks_kernel,
        out_shape=[block] * 4,
        in_specs=[SMEM] + [VMEM] * 5,
        out_specs=[VMEM] * 4,
        compiler_params=PARAMS,
        name="blocks",
    )(info, part, states[STEPS - 1], snapshots[0], states[0], snapshots[STEPS - 1])
    keep = give = jnp.zeros((ROWS, TILE, DEPTH), F32)
    for shift in range(half):
        arrived = blocks[0] if shift == 0 else lax.ppermute(blocks[shift], "shot", ring_pairs(shift))
        mine = tile_of(upper * half + (ring - shift) % half) == upper
        keep = keep + jnp.where(mine, arrived, 0.0)
        give = give + jnp.where(mine, 0.0, arrived)
    image = keep + lax.ppermute(give, "shot", side_pairs)
    return image, states[STEPS - 1][None]


def solution(mesh):
    placed = (
        P("shot", "apert", None, None),
        P("shot", "apert", None, None),
        P("shot", "apert", None, None),
        P("shot", "apert", None, None),
        P("apert", "shot", None),
        P("apert", "shot", None),
        P("shot"),
        P("shot"),
        P("shot", None),
        P("shot", None, "apert", None),
    )
    return jax.shard_map(
        shards,
        mesh=mesh,
        in_specs=placed,
        out_specs=(P("apert", "shot", None), P("shot", "apert", None, None)),
        check_vma=False,
    )
```

time: 892 us -> 349 us (0.39)
  other arithmetic: 474 us -> 11.5 us
  local copies, waits for them, and re-layouts: 192 us -> 20.1 us
  Pallas kernels: 0 us -> 150 us
  starting transfers between devices: 111 us -> 75.3 us
  waiting for transfers between devices: 90.6 us -> 58 us
  blocking collectives: 0 us -> 9.69 us
    add x12 -> x3, other arithmetic: 469 us -> 5.78 us  [the longest x1 3.53 us: shards(): sum((states[t] * snapshots[STEPS - 1 - t] for t in range(1, STEPS - 1)))]
    pallas_call x0 -> x15, Pallas kernels: none -> 150 us  [the longest x12 134 us: step(): pl.pallas_call(functools.partial(step_kernel, mode, first), out_shape=out...]
    slice x36 -> x1, local copies, waits for them, and re-layouts: 76.8 us -> 0.68 us  [shards(): wavelet[0, moment:moment + 1]]
    ppermute x26 -> x0, local copies, waits for them, and re-layouts: 61.6 us -> none  [the longest x13 31.5 us: extended_2(): lax.ppermute(lax.slice_in_dim(block, block.shape[dim] - width, None, axis...]
    ppermute x26 -> x34, waiting for transfers between devices: 0.07 us -> 58 us  [the longest x13 25.1 us: swap(): lax.ppermute(cross, 'apert', cross_pairs)]
    all_gather x2 -> x0, waiting for transfers between devices: 46.7 us -> none  [the longest x1 24.9 us: shards(): lax.all_gather(density, 'shot', axis=1, tiled=True)]
    all_to_all x1 -> x0, waiting for transfers between devices: 43.7 us -> none  [shards(): lax.all_to_all(blocks, 'shot', split_axis=0, concat_axis=0, tiled=True)]
    ppermute x26 -> x34, starting transfers between devices: 104 us -> 75.3 us  [the longest x13 52 us: swap(): lax.ppermute(cross, 'apert', cross_pairs)]
  transfers between devices with their start and end apart: 29 -> 34, of which waited for: 3 -> 10; matrix products, arithmetic and copies ran while one was open for 53% -> 5% of each run, Pallas kernels for 0% -> 39%
where the time goes in v1:
time: 349 us; the launch traced here: 345 us
  Pallas kernels  150 us (43%)
  starting transfers between devices  75.3 us (22%)
  waiting for transfers between devices  58 us (17%)
  between operations  20.8 us (6%)
  local copies, waits for them, and re-layouts  20.1 us (6%)
  other arithmetic  11.5 us (3%)
  blocking collectives  9.69 us (3%)
    pallas_call x12, Pallas kernels, step(): pl.pallas_call(functools.partial(step_kernel, mode, first), out_shape=out...  134 us
    ppermute x13, starting transfers between devices, swap(): lax.ppermute(cross, 'apert', cross_pairs)  52 us
    ppermute x13, waiting for transfers between devices, swap(): lax.ppermute(cross, 'apert', cross_pairs)  25.1 us
    ppermute x13, starting transfers between devices, swap(): lax.ppermute(core, 'apert', core_pairs)  16.2 us
    ppermute x3, waiting for transfers between devices, shards(): lax.ppermute(blocks[shift], 'shot', ring_pairs(shift))  15.7 us
    unnamed x85, local copies, waits for them, and re-layouts  13 us
    ppermute x1, waiting for transfers between devices, shards(): image = keep + lax.ppermute(give, 'shot', side_pairs)  11.8 us
    unnamed x1, blocking collectives  9.69 us
  transfers between devices with their start and end apart: 34, of which 10 were waited for; matrix products, arithmetic and copies ran while one was open for 5% of the time, Pallas kernels for 39%

profile of v1, /device:TPU:7, one launch (start us, length us, event | category | flops | bytes accessed | tf_op | source)
XLA Modules:
  0.0 345.4 jit_solution(4270964582911378140)
XLA Ops:
  5.1 9.7 %all-reduce = s32[8]{0:T(128)S(1)} all-reduce(s32[8]{0:T(128)S(1)} %dynamic-update-slice), channel_id=1, replica_groups=mesh['shot'=8,'apert'=16] {'shot'}, use_global_device_ids=true, to_apply=%add | all-reduce | flops 8 | bytes 64
  34.5 4.3 %collective-permute-start.11 = (f32[4,160,256]{2,1,0:T(8,128)S(1)}, f32[4,160,256]{2,1,0:T(8,128)}, u32[]{:S(2)}, u32[]{:S(2)}) collective-permute-start(f32[4,160,256]{2,1,0:T(8,128)S(1)} %get-tuple-element.132.refs_9_), channel_id=1, source_target_pairs={{1,2},{3,4},{5,6},{7,8},{9,10},{11,12},{13,14},{2,1},{4,3},{6,5},{... | collective-permute-start | bytes 1966088 | tf_op jit(solution)/shard_map/ppermute | solution.py:278
  42.7 11.1 %collective-permute-start = (f32[4,160,256]{2,1,0:T(8,128)}, f32[4,160,256]{2,1,0:T(8,128)S(1)}, u32[]{:S(2)}, u32[]{:S(2)}) collective-permute-start(f32[4,160,256]{2,1,0:T(8,128)} %get-tuple-element.135), channel_id=1, source_target_pairs={{0,1},{1,0},{2,3},{3,2},{4,5},{5,4},{6,7},{7,6},{8,9},{9,8},{10,11... | collective-permute-start | bytes 1966088 | tf_op jit(solution)/shard_map/ppermute | solution.py:278
  60.9 4.3 %collective-permute-start.7 = (bf16[4,160,256]{2,1,0:T(8,128)(2,1)}, bf16[4,160,256]{2,1,0:T(8,128)(2,1)}, u32[]{:S(2)}, u32[]{:S(2)}) collective-permute-start(bf16[4,160,256]{2,1,0:T(8,128)(2,1)} %get-tuple-element.67), channel_id=1, source_target_pairs={{1,2},{3,4},{5,6},{7,8},{9,10},{11,12},{13,14},{2,1},{4,3},{6,5},{... | collective-permute-start | bytes 983048 | tf_op jit(solution)/shard_map/ppermute | solution.py:278
  75.3 8.2 %slopes.1 = (f32[8,160,256]{2,1,0:T(8,128)}, f32[8,160,256]{2,1,0:T(8,128)}, f32[8,160,256]{2,1,0:T(8,128)}, f32[8,160,256]{2,1,0:T(8,128)}) custom-call(s32[2]{0:T(128)} %pad_add_fusion.info, f32[8,160,256]{2,1,0:T(8,128)} %get-tuple-element.64.vel, bf16[8,160,256]{2,1,0:T(8,128)(2,1)} %get-tuple-element.65.dens, bf16[4,160,256]{2,1,0:T(8,128)(2,1)} %copy-done.34, ...), custom_call_target="tpu_custom_call" | custom-call | tf_op jit(solution)/shard_map/slopes/pallas_call | solution.py:319
  84.3 11.4 %step_fwd.6 = (f32[8,160,256]{2,1,0:T(8,128)}, f32[4,160,256]{2,1,0:T(8,128)}, bf16[4,160,256]{2,1,0:T(8,128)(2,1)}, f32[4,160,256]{2,1,0:T(8,128)}, f32[4,160,256]{2,1,0:T(8,128)}) custom-call(s32[6]{0:T(128)} %stack.88.refs_0_, f32[1]{0:T(128)} %bitcast.32.refs_1_, f32[8,160,256]{2,1,0:T(8,128)} %bitcast.74, f32[8,160,256]{2,1,0:T(8,128)} %bitcast.69, ...), custom_call_target="tpu_custom_call" | custom-call | flops 1500000000 | bytes 12000000 | tf_op jit(solution)/shard_map/step_fwd/pallas_call | solution.py:195
  98.7 10.5 %step_bwd.6 = (f32[8,160,256]{2,1,0:T(8,128)}, f32[4,160,256]{2,1,0:T(8,128)}, bf16[4,160,256]{2,1,0:T(8,128)(2,1)}, f32[4,160,256]{2,1,0:T(8,128)}, f32[4,160,256]{2,1,0:T(8,128)}) custom-call(s32[6]{0:T(128)} %stack.88.refs_0_, f32[8,160,256]{2,1,0:T(8,128)} %bitcast.75, f32[8,160,256]{2,1,0:T(8,128)} %bitcast.71, f32[4,160,256]{2,1,0:T(8,128)} %copy-done.15, ...), custom_call_target="tpu_custom_call" | custom-call | flops 1500000000 | bytes 12000000 | tf_op jit(solution)/shard_map/step_bwd/pallas_call | solution.py:195
  117.6 6.3 %collective-permute-done.13.refs_5_ = bf16[4,160,256]{2,1,0:T(8,128)(2,1)S(1)} collective-permute-done((bf16[4,160,256]{2,1,0:T(8,128)(2,1)S(1)}, bf16[4,160,256]{2,1,0:T(8,128)(2,1)S(1)}, u32[]{:S(2)}, u32[]{:S(2)}) %collective-permute-start.13) | collective-permute-done | bytes 327712 | tf_op jit(solution)/shard_map/ppermute | solution.py:278
  124.9 11.4 %step_fwd.7 = (f32[8,160,256]{2,1,0:T(8,128)}, f32[4,160,256]{2,1,0:T(8,128)}, bf16[4,160,256]{2,1,0:T(8,128)(2,1)}, f32[4,160,256]{2,1,0:T(8,128)}, f32[4,160,256]{2,1,0:T(8,128)}) custom-call(s32[6]{0:T(128)} %stack.88.refs_0_, f32[1]{0:T(128)} %bitcast.37.refs_1_, f32[8,160,256]{2,1,0:T(8,128)} %bitcast.70, ...), custom_call_target="tpu_custom_call" | custom-call | flops 1500000000 | bytes 12000000 | tf_op jit(solution)/shard_map/step_fwd/pallas_call | solution.py:195
  137.3 11.2 %step_bwd.7 = (f32[8,160,256]{2,1,0:T(8,128)}, f32[4,160,256]{2,1,0:T(8,128)}, bf16[4,160,256]{2,1,0:T(8,128)(2,1)}, f32[4,160,256]{2,1,0:T(8,128)}, f32[4,160,256]{2,1,0:T(8,128)}) custom-call(s32[6]{0:T(128)} %stack.88.refs_0_, f32[8,160,256]{2,1,0:T(8,128)} %bitcast.72, f32[8,160,256]{2,1,0:T(8,128)} %get-tuple-element.72.refs_2_.refs_1_.a0, ...), custom_call_target="tpu_custom_call" | custom-call | flops 1500000000 | bytes 12000000 | tf_op jit(solution)/shard_map/step_bwd/pallas_call | solution.py:195
  156.9 6.3 %collective-permute-done.15.refs_5_ = bf16[4,160,256]{2,1,0:T(8,128)(2,1)S(1)} collective-permute-done((bf16[4,160,256]{2,1,0:T(8,128)(2,1)S(1)}, bf16[4,160,256]{2,1,0:T(8,128)(2,1)S(1)}, u32[]{:S(2)}, u32[]{:S(2)}) %collective-permute-start.15) | collective-permute-done | bytes 327712 | tf_op jit(solution)/shard_map/ppermute | solution.py:278
  164.3 11.6 %step_fwd.8 = (f32[8,160,256]{2,1,0:T(8,128)}, f32[4,160,256]{2,1,0:T(8,128)}, bf16[4,160,256]{2,1,0:T(8,128)(2,1)}, f32[4,160,256]{2,1,0:T(8,128)}, f32[4,160,256]{2,1,0:T(8,128)}) custom-call(s32[6]{0:T(128)} %stack.88.refs_0_, f32[1]{0:T(128)} %bitcast.31.refs_1_, f32[8,160,256]{2,1,0:T(8,128)} %get-tuple-element.78.refs_3_.refs_2_.s0, ...), custom_call_target="tpu_custom_call" | custom-call | flops 1500000000 | bytes 12000000 | tf_op jit(solution)/shard_map/step_fwd/pallas_call | solution.py:195
  176.8 11.2 %step_bwd.8 = (f32[8,160,256]{2,1,0:T(8,128)}, f32[4,160,256]{2,1,0:T(8,128)}, bf16[4,160,256]{2,1,0:T(8,128)(2,1)}, f32[4,160,256]{2,1,0:T(8,128)}, f32[4,160,256]{2,1,0:T(8,128)}) custom-call(s32[6]{0:T(128)} %stack.88.refs_0_, f32[8,160,256]{2,1,0:T(8,128)} %get-tuple-element.72.refs_2_.refs_1_.a0, f32[8,160,256]{2,1,0:T(8,128)} %get-tuple-element.77.refs_2_.refs_1_, ...), custom_call_target="tpu_custom_call" | custom-call | flops 1500000000 | bytes 12000000 | tf_op jit(solution)/shard_map/step_bwd/pallas_call | solution.py:195
  196.4 6.2 %collective-permute-done.17.refs_5_ = bf16[4,160,256]{2,1,0:T(8,128)(2,1)S(1)} collective-permute-done((bf16[4,160,256]{2,1,0:T(8,128)(2,1)S(1)}, bf16[4,160,256]{2,1,0:T(8,128)(2,1)S(1)}, u32[]{:S(2)}, u32[]{:S(2)}) %collective-permute-start.17) | collective-permute-done | bytes 327712 | tf_op jit(solution)/shard_map/ppermute | solution.py:278
  203.6 11.5 %step_fwd.9 = (f32[8,160,256]{2,1,0:T(8,128)}, f32[4,160,256]{2,1,0:T(8,128)}, bf16[4,160,256]{2,1,0:T(8,128)(2,1)}, f32[4,160,256]{2,1,0:T(8,128)}, f32[4,160,256]{2,1,0:T(8,128)}) custom-call(s32[6]{0:T(128)} %stack.88.refs_0_, f32[1]{0:T(128)} %bitcast.38.refs_1_, f32[8,160,256]{2,1,0:T(8,128)} %get-tuple-element.83.refs_3_.refs_2_, ...), custom_call_target="tpu_custom_call" | custom-call | flops 1500000000 | bytes 12000000 | tf_op jit(solution)/shard_map/step_fwd/pallas_call | solution.py:195
  216.1 11.1 %step_bwd.9 = (f32[8,160,256]{2,1,0:T(8,128)}, f32[4,160,256]{2,1,0:T(8,128)}, bf16[4,160,256]{2,1,0:T(8,128)(2,1)}, f32[4,160,256]{2,1,0:T(8,128)}, f32[4,160,256]{2,1,0:T(8,128)}) custom-call(s32[6]{0:T(128)} %stack.88.refs_0_, f32[8,160,256]{2,1,0:T(8,128)} %get-tuple-element.77.refs_2_.refs_1_, f32[8,160,256]{2,1,0:T(8,128)} %get-tuple-element.103.refs_2_.refs_1_, ...), custom_call_target="tpu_custom_call" | custom-call | flops 1500000000 | bytes 12000000 | tf_op jit(solution)/shard_map/step_bwd/pallas_call | solution.py:195
  236.4 5.7 %collective-permute-done.19.refs_5_ = bf16[4,160,256]{2,1,0:T(8,128)(2,1)S(1)} collective-permute-done((bf16[4,160,256]{2,1,0:T(8,128)(2,1)S(1)}, bf16[4,160,256]{2,1,0:T(8,128)(2,1)S(1)}, u32[]{:S(2)}, u32[]{:S(2)}) %collective-permute-start.19) | collective-permute-done | bytes 327712 | tf_op jit(solution)/shard_map/ppermute | solution.py:278
  243.0 11.5 %step_fwd.10 = (f32[8,160,256]{2,1,0:T(8,128)}, f32[4,160,256]{2,1,0:T(8,128)}, bf16[4,160,256]{2,1,0:T(8,128)(2,1)}, f32[4,160,256]{2,1,0:T(8,128)}, f32[4,160,256]{2,1,0:T(8,128)}) custom-call(s32[6]{0:T(128)} %stack.88.refs_0_, f32[1]{0:T(128)} %bitcast.30.refs_1_, f32[8,160,256]{2,1,0:T(8,128)} %get-tuple-element.88.refs_3_.refs_2_, ...), custom_call_target="tpu_custom_call" | custom-call | flops 1500000000 | bytes 12000000 | tf_op jit(solution)/shard_map/step_fwd/pallas_call | solution.py:195
  259.3 11.2 %step_bwd.10 = (f32[8,160,256]{2,1,0:T(8,128)}, f32[4,160,256]{2,1,0:T(8,128)}, bf16[4,160,256]{2,1,0:T(8,128)(2,1)}, f32[4,160,256]{2,1,0:T(8,128)}, f32[4,160,256]{2,1,0:T(8,128)}) custom-call(s32[6]{0:T(128)} %stack.88.refs_0_, f32[8,160,256]{2,1,0:T(8,128)} %get-tuple-element.103.refs_2_.refs_1_, f32[8,160,256]{2,1,0:T(8,128)} %get-tuple-element.108.refs_2_.refs_1_, ...), custom_call_target="tpu_custom_call" | custom-call | flops 1500000000 | bytes 12000000 | tf_op jit(solution)/shard_map/step_bwd/pallas_call | solution.py:195
  278.4 10.7 %step_fwd.11.s5 = f32[8,160,256]{2,1,0:T(8,128)} custom-call(s32[6]{0:T(128)} %stack.88.refs_0_, f32[1]{0:T(128)} %bitcast.43.refs_1_, f32[8,160,256]{2,1,0:T(8,128)} %get-tuple-element.93.refs_3_.refs_2_, f32[8,160,256]{2,1,0:T(8,128)} %get-tuple-element.98.refs_3_, f32[4,160,256]{2,1,0:T(8,128)} %collective-permute-done.28.refs_4_, ...), custom_call_target="tpu_custom_call" | custom-call | flops 1500000000 | bytes 12000000 | tf_op jit(solution)/shard_map/step_fwd/pallas_call | solution.py:195
  289.9 10.4 %step_bwd.11.a5 = f32[8,160,256]{2,1,0:T(8,128)} custom-call(s32[6]{0:T(128)} %stack.88.refs_0_, f32[8,160,256]{2,1,0:T(8,128)} %get-tuple-element.108.refs_2_.refs_1_, f32[8,160,256]{2,1,0:T(8,128)} %get-tuple-element.113.refs_2_, f32[4,160,256]{2,1,0:T(8,128)} %collective-permute-done.26.refs_3_, bf16[4,160,256]{2,1,0:T(8,128)(2,1)} %copy-done.27, ...), custom_call_target="tpu_custom_call" | custom-call | flops 1500000000 | bytes 12000000 | tf_op jit(solution)/shard_map/step_bwd/pallas_call | solution.py:195
  300.2 5.0 %blocks.1 = (f32[8,64,256]{2,1,0:T(8,128)}, f32[8,64,256]{2,1,0:T(8,128)}, f32[8,64,256]{2,1,0:T(8,128)}, f32[8,64,256]{2,1,0:T(8,128)}) custom-call(s32[5]{0:T(128)} %stack.79.info, f32[8,160,256]{2,1,0:T(8,128)} %multiply_add_fusion.part, f32[8,160,256]{2,1,0:T(8,128)} %step_bwd.11.a5, f32[8,160,256]{2,1,0:T(8,128)} %get-tuple-element.78.refs_3_.refs_2_.s0, ...), custom_call_target="tpu_custom_call" | custom-call | tf_op jit(solution)/shard_map/blocks/pallas_call | solution.py:377
  315.6 15.3 %collective-permute-done.30 = f32[8,64,256]{2,1,0:T(8,128)S(1)} collective-permute-done((f32[8,64,256]{2,1,0:T(8,128)}, f32[8,64,256]{2,1,0:T(8,128)S(1)}, u32[]{:S(2)}, u32[]{:S(2)}) %collective-permute-start.30) | collective-permute-done | bytes 524320 | tf_op jit(solution)/shard_map/ppermute | solution.py:387
  332.6 11.8 %collective-permute-done.33 = f32[8,64,256]{2,1,0:T(8,128)S(1)} collective-permute-done((f32[8,64,256]{2,1,0:T(8,128)S(1)}, f32[8,64,256]{2,1,0:T(8,128)S(1)}, u32[]{:S(2)}, u32[]{:S(2)}) %collective-permute-start.33) | collective-permute-done | bytes 524320 | tf_op jit(solution)/shard_map/ppermute | solution.py:391
  (161 shorter events, 97.0 us)
Async XLA Ops:
  1.8 24.1 %collective-permute-start.2 = (bf16[2,8,64,256]{3,2,1,0:T(8,128)(2,1)S(1)}, bf16[2,8,64,256]{3,2,1,0:T(8,128)(2,1)S(1)}, u32[]{:S(2)}, u32[]{:S(2)}) collective-permute-start(bf16[2,8,64,256]{3,2,1,0:T(8,128)(2,1)S(1)} %pad_maximum_fusion), channel_id=1, source_target_pairs={{0,64},{16,80},{32,96},{48,112},{64,0},{80,16},{96,32},{112,48},{1... | collective-permute-start | bytes 1572872 | tf_op jit(solution)/shard_map/ppermute | solution.py:282
  30.1 23.7 %collective-permute-start.4 = (bf16[2,8,64,256]{3,2,1,0:T(8,128)(2,1)}, bf16[2,8,64,256]{3,2,1,0:T(8,128)(2,1)}, u32[]{:S(2)}, u32[]{:S(2)}) collective-permute-start(bf16[2,8,64,256]{3,2,1,0:T(8,128)(2,1)} %get-tuple-element.137), channel_id=1, source_target_pairs={{0,32},{16,48},{32,0},{48,16},{64,96},{80,112},{96,64},{112,80},{1... | collective-permute-start | bytes 1572872 | tf_op jit(solution)/shard_map/ppermute | solution.py:294
  30.4 26.6 %collective-permute-start.3 = (bf16[2,8,64,256]{3,2,1,0:T(8,128)(2,1)}, bf16[2,8,64,256]{3,2,1,0:T(8,128)(2,1)}, u32[]{:S(2)}, u32[]{:S(2)}) collective-permute-start(bf16[2,8,64,256]{3,2,1,0:T(8,128)(2,1)} %get-tuple-element.138), channel_id=1, source_target_pairs={{0,16},{16,32},{32,48},{48,0},{64,80},{80,96},{96,112},{112,64},{1... | collective-permute-start | bytes 1572872 | tf_op jit(solution)/shard_map/ppermute | solution.py:294
  32.2 51.3 %collective-permute-start.10 = (f32[4,160,256]{2,1,0:T(8,128)}, f32[4,160,256]{2,1,0:T(8,128)S(1)}, u32[]{:S(2)}, u32[]{:S(2)}) collective-permute-start(f32[4,160,256]{2,1,0:T(8,128)} %get-tuple-element.133), channel_id=1, source_target_pairs={{0,1},{1,0},{2,3},{3,2},{4,5},{5,4},{6,7},{7,6},{8,9},{9,8},{10,11... | collective-permute-start | bytes 1966088 | tf_op jit(solution)/shard_map/ppermute | solution.py:278
  34.5 48.9 %collective-permute-start.11 = (f32[4,160,256]{2,1,0:T(8,128)S(1)}, f32[4,160,256]{2,1,0:T(8,128)}, u32[]{:S(2)}, u32[]{:S(2)}) collective-permute-start(f32[4,160,256]{2,1,0:T(8,128)S(1)} %get-tuple-element.132.refs_9_), channel_id=1, source_target_pairs={{1,2},{3,4},{5,6},{7,8},{9,10},{11,12},{13,14},{2,1},{4,3},{6,5},{... | collective-permute-start | bytes 1966088 | tf_op jit(solution)/shard_map/ppermute | solution.py:278
  42.7 55.0 %collective-permute-start = (f32[4,160,256]{2,1,0:T(8,128)}, f32[4,160,256]{2,1,0:T(8,128)S(1)}, u32[]{:S(2)}, u32[]{:S(2)}) collective-permute-start(f32[4,160,256]{2,1,0:T(8,128)} %get-tuple-element.135), channel_id=1, source_target_pairs={{0,1},{1,0},{2,3},{3,2},{4,5},{5,4},{6,7},{7,6},{8,9},{9,8},{10,11... | collective-permute-start | bytes 1966088 | tf_op jit(solution)/shard_map/ppermute | solution.py:278
  69.8 27.9 %collective-permute-start.1 = (f32[4,160,256]{2,1,0:T(8,128)S(1)}, f32[4,160,256]{2,1,0:T(8,128)S(1)}, u32[]{:S(2)}, u32[]{:S(2)}) collective-permute-start(f32[4,160,256]{2,1,0:T(8,128)S(1)} %get-tuple-element.134.refs_8_), channel_id=1, source_target_pairs={{1,2},{3,4},{5,6},{7,8},{9,10},{11,12},{13,14},{2,1},{4,3},{6,5},{... | collective-permute-start | bytes 1966088 | tf_op jit(solution)/shard_map/ppermute | solution.py:278
  95.7 28.3 %collective-permute-start.12 = (f32[4,160,256]{2,1,0:T(8,128)}, f32[4,160,256]{2,1,0:T(8,128)S(1)}, u32[]{:S(2)}, u32[]{:S(2)}) collective-permute-start(f32[4,160,256]{2,1,0:T(8,128)} %get-tuple-element.79), channel_id=1, source_target_pairs={{0,1},{1,0},{2,3},{3,2},{4,5},{5,4},{6,7},{7,6},{8,9},{9,8},{10,11... | collective-permute-start | bytes 1966088 | tf_op jit(solution)/shard_map/ppermute | solution.py:278
  109.2 27.2 %collective-permute-start.8 = (f32[4,160,256]{2,1,0:T(8,128)}, f32[4,160,256]{2,1,0:T(8,128)S(1)}, u32[]{:S(2)}, u32[]{:S(2)}) collective-permute-start(f32[4,160,256]{2,1,0:T(8,128)} %get-tuple-element.73), channel_id=1, source_target_pairs={{0,1},{1,0},{2,3},{3,2},{4,5},{5,4},{6,7},{7,6},{8,9},{9,8},{10,11... | collective-permute-start | bytes 1966088 | tf_op jit(solution)/shard_map/ppermute | solution.py:278
  113.5 22.9 %collective-permute-start.9 = (bf16[4,160,256]{2,1,0:T(8,128)(2,1)}, bf16[4,160,256]{2,1,0:T(8,128)(2,1)S(1)}, u32[]{:S(2)}, u32[]{:S(2)}) collective-permute-start(bf16[4,160,256]{2,1,0:T(8,128)(2,1)} %get-tuple-element.74), channel_id=1, source_target_pairs={{1,2},{3,4},{5,6},{7,8},{9,10},{11,12},{13,14},{2,1},{4,3},{6,5},{... | collective-permute-start | bytes 983048 | tf_op jit(solution)/shard_map/ppermute | solution.py:278
  136.3 26.9 %collective-permute-start.14 = (f32[4,160,256]{2,1,0:T(8,128)}, f32[4,160,256]{2,1,0:T(8,128)S(1)}, u32[]{:S(2)}, u32[]{:S(2)}) collective-permute-start(f32[4,160,256]{2,1,0:T(8,128)} %get-tuple-element.84), channel_id=1, source_target_pairs={{0,1},{1,0},{2,3},{3,2},{4,5},{5,4},{6,7},{7,6},{8,9},{9,8},{10,11... | collective-permute-start | bytes 1966088 | tf_op jit(solution)/shard_map/ppermute | solution.py:278
  148.5 27.4 %collective-permute-start.20 = (f32[4,160,256]{2,1,0:T(8,128)}, f32[4,160,256]{2,1,0:T(8,128)S(1)}, u32[]{:S(2)}, u32[]{:S(2)}) collective-permute-start(f32[4,160,256]{2,1,0:T(8,128)} %get-tuple-element.99), channel_id=1, source_target_pairs={{0,1},{1,0},{2,3},{3,2},{4,5},{5,4},{6,7},{7,6},{8,9},{9,8},{10,11... | collective-permute-start | bytes 1966088 | tf_op jit(solution)/shard_map/ppermute | solution.py:278
  152.9 23.0 %collective-permute-start.21 = (bf16[4,160,256]{2,1,0:T(8,128)(2,1)}, bf16[4,160,256]{2,1,0:T(8,128)(2,1)S(1)}, u32[]{:S(2)}, u32[]{:S(2)}) collective-permute-start(bf16[4,160,256]{2,1,0:T(8,128)(2,1)} %get-tuple-element.100), channel_id=1, source_target_pairs={{1,2},{3,4},{5,6},{7,8},{9,10},{11,12},{13,14},{2,1},{4,3},{6,5},{... | collective-permute-start | bytes 983048 | tf_op jit(solution)/shard_map/ppermute | solution.py:278
  175.8 26.9 %collective-permute-start.16 = (f32[4,160,256]{2,1,0:T(8,128)}, f32[4,160,256]{2,1,0:T(8,128)S(1)}, u32[]{:S(2)}, u32[]{:S(2)}) collective-permute-start(f32[4,160,256]{2,1,0:T(8,128)} %get-tuple-element.89), channel_id=1, source_target_pairs={{0,1},{1,0},{2,3},{3,2},{4,5},{5,4},{6,7},{7,6},{8,9},{9,8},{10,11... | collective-permute-start | bytes 1966088 | tf_op jit(solution)/shard_map/ppermute | solution.py:278
  188.0 27.2 %collective-permute-start.22 = (f32[4,160,256]{2,1,0:T(8,128)}, f32[4,160,256]{2,1,0:T(8,128)S(1)}, u32[]{:S(2)}, u32[]{:S(2)}) collective-permute-start(f32[4,160,256]{2,1,0:T(8,128)} %get-tuple-element.104), channel_id=1, source_target_pairs={{0,1},{1,0},{2,3},{3,2},{4,5},{5,4},{6,7},{7,6},{8,9},{9,8},{10,11... | collective-permute-start | bytes 1966088 | tf_op jit(solution)/shard_map/ppermute | solution.py:278
  192.2 23.0 %collective-permute-start.23 = (bf16[4,160,256]{2,1,0:T(8,128)(2,1)}, bf16[4,160,256]{2,1,0:T(8,128)(2,1)S(1)}, u32[]{:S(2)}, u32[]{:S(2)}) collective-permute-start(bf16[4,160,256]{2,1,0:T(8,128)(2,1)} %get-tuple-element.105), channel_id=1, source_target_pairs={{1,2},{3,4},{5,6},{7,8},{9,10},{11,12},{13,14},{2,1},{4,3},{6,5},{... | collective-permute-start | bytes 983048 | tf_op jit(solution)/shard_map/ppermute | solution.py:278
  215.1 26.9 %collective-permute-start.18 = (f32[4,160,256]{2,1,0:T(8,128)}, f32[4,160,256]{2,1,0:T(8,128)S(1)}, u32[]{:S(2)}, u32[]{:S(2)}) collective-permute-start(f32[4,160,256]{2,1,0:T(8,128)} %get-tuple-element.94), channel_id=1, source_target_pairs={{0,1},{1,0},{2,3},{3,2},{4,5},{5,4},{6,7},{7,6},{8,9},{9,8},{10,11... | collective-permute-start | bytes 1966088 | tf_op jit(solution)/shard_map/ppermute | solution.py:278
  227.2 31.1 %collective-permute-start.24 = (f32[4,160,256]{2,1,0:T(8,128)}, f32[4,160,256]{2,1,0:T(8,128)S(1)}, u32[]{:S(2)}, u32[]{:S(2)}) collective-permute-start(f32[4,160,256]{2,1,0:T(8,128)} %get-tuple-element.109), channel_id=1, source_target_pairs={{0,1},{1,0},{2,3},{3,2},{4,5},{5,4},{6,7},{7,6},{8,9},{9,8},{10,11... | collective-permute-start | bytes 1966088 | tf_op jit(solution)/shard_map/ppermute | solution.py:278
  231.6 26.7 %collective-permute-start.25 = (bf16[4,160,256]{2,1,0:T(8,128)(2,1)}, bf16[4,160,256]{2,1,0:T(8,128)(2,1)S(1)}, u32[]{:S(2)}, u32[]{:S(2)}) collective-permute-start(bf16[4,160,256]{2,1,0:T(8,128)(2,1)} %get-tuple-element.110), channel_id=1, source_target_pairs={{1,2},{3,4},{5,6},{7,8},{9,10},{11,12},{13,14},{2,1},{4,3},{6,5},{... | collective-permute-start | bytes 983048 | tf_op jit(solution)/shard_map/ppermute | solution.py:278
  254.5 23.9 %collective-permute-start.29 = (bf16[4,160,256]{2,1,0:T(8,128)(2,1)}, bf16[4,160,256]{2,1,0:T(8,128)(2,1)}, u32[]{:S(2)}, u32[]{:S(2)}) collective-permute-start(bf16[4,160,256]{2,1,0:T(8,128)(2,1)} %get-tuple-element.119), channel_id=1, source_target_pairs={{1,2},{3,4},{5,6},{7,8},{9,10},{11,12},{13,14},{2,1},{4,3},{6,5},{... | collective-permute-start | bytes 983048 | tf_op jit(solution)/shard_map/ppermute | solution.py:278
  258.2 20.2 %collective-permute-start.28 = (f32[4,160,256]{2,1,0:T(8,128)}, f32[4,160,256]{2,1,0:T(8,128)}, u32[]{:S(2)}, u32[]{:S(2)}) collective-permute-start(f32[4,160,256]{2,1,0:T(8,128)} %get-tuple-element.118), channel_id=1, source_target_pairs={{0,1},{1,0},{2,3},{3,2},{4,5},{5,4},{6,7},{7,6},{8,9},{9,8},{10,11... | collective-permute-start | bytes 1966088 | tf_op jit(solution)/shard_map/ppermute | solution.py:278
  305.2 25.7 %collective-permute-start.30 = (f32[8,64,256]{2,1,0:T(8,128)}, f32[8,64,256]{2,1,0:T(8,128)S(1)}, u32[]{:S(2)}, u32[]{:S(2)}) collective-permute-start(f32[8,64,256]{2,1,0:T(8,128)} %get-tuple-element.123), channel_id=1, source_target_pairs={{0,16},{16,32},{32,48},{48,0},{64,80},{80,96},{96,112},{112,64},{1... | collective-permute-start | bytes 1572872 | tf_op jit(solution)/shard_map/ppermute | solution.py:387
  305.2 25.7 %collective-permute-start.31 = (f32[8,64,256]{2,1,0:T(8,128)}, f32[8,64,256]{2,1,0:T(8,128)S(1)}, u32[]{:S(2)}, u32[]{:S(2)}) collective-permute-start(f32[8,64,256]{2,1,0:T(8,128)} %get-tuple-element.124), channel_id=1, source_target_pairs={{0,32},{16,48},{32,0},{48,16},{64,96},{80,112},{96,64},{112,80},{1... | collective-permute-start | bytes 1572872 | tf_op jit(solution)/shard_map/ppermute | solution.py:387
  306.7 24.5 %collective-permute-start.32 = (f32[8,64,256]{2,1,0:T(8,128)}, f32[8,64,256]{2,1,0:T(8,128)S(1)}, u32[]{:S(2)}, u32[]{:S(2)}) collective-permute-start(f32[8,64,256]{2,1,0:T(8,128)} %get-tuple-element.125), channel_id=1, source_target_pairs={{0,48},{16,0},{32,16},{48,32},{64,112},{80,64},{96,80},{112,96},{1... | collective-permute-start | bytes 1572872 | tf_op jit(solution)/shard_map/ppermute | solution.py:387
  (51 other events, 457.7 us)

commit v2 on v1

v2 whole, which is shorter than its diff:
```python
import functools

import jax
import jax.numpy as jnp
import ml_dtypes
import numpy as np
from jax import lax
from jax.experimental import pallas as pl
from jax.experimental.pallas import tpu as pltpu
from jax.sharding import PartitionSpec as P

STEPS = 6
SURF = 8
ROWS, COLS, DEPTH = 8, 160, 256
TILE = 64
LAP = (-14350.0, 8064.0, -1008.0, 128.0, -9.0)
SLOPE = (672.0, -168.0, 32.0, -3.0)
LAP_SCALE, SLOPE_SCALE = 1.0 / 5040.0, 1.0 / 840.0
F32, BF16 = jnp.float32, jnp.bfloat16
VMEM = pl.BlockSpec(memory_space=pltpu.VMEM)
SMEM = pl.BlockSpec(memory_space=pltpu.SMEM)
PARAMS = pltpu.CompilerParams(vmem_limit_bytes=16 * 1024 * 1024)


def banded(size):
    lap, slope = np.zeros((size, size)), np.zeros((size, size))
    for k in range(1, 5):
        lap += LAP[k] * (np.eye(size, k=k) + np.eye(size, k=-k))
        slope += SLOPE[k - 1] * (np.eye(size, k=k) - np.eye(size, k=-k))
    return lap, slope


def weight_tables():
    lap, slope = banded(DEPTH)
    depth_table = np.concatenate([lap.T, slope.T], axis=1).astype(ml_dtypes.bfloat16)
    lap, slope = banded(COLS)
    cols_table = np.concatenate([lap, slope], axis=0).astype(ml_dtypes.bfloat16)
    return jnp.asarray(depth_table), jnp.asarray(cols_table)


def halves(x):
    high = x.astype(BF16)
    return high, (x - high.astype(F32)).astype(BF16)


def in_plane(src, depth_w, cols_w, zz, cc):
    def body(r, carry):
        high, low = halves(src[4 + r])
        zz[r] = jnp.dot(high, depth_w[...], preferred_element_type=F32) + jnp.dot(
            low, depth_w[...], preferred_element_type=F32
        )
        cc[r] = jnp.dot(cols_w[...], high, preferred_element_type=F32) + jnp.dot(
            cols_w[...], low, preferred_element_type=F32
        )
        return carry

    lax.fori_loop(0, ROWS, body, 0)


def load_extended(ext, now, parity, core_rows, cross_rows):
    ext[4 : 4 + ROWS] = now[...]
    core_at = pl.multiple_of((1 - parity) * 12, 4)
    cross_at = pl.multiple_of(parity * 12, 4)
    ext[pl.ds(core_at, 4)] = core_rows
    ext[pl.ds(cross_at, 4)] = cross_rows


def call(body, args, outs, scratch=(), name=None):
    specs, given = [], []
    for arg in args:
        if arg.ndim == 1:
            specs.append(SMEM)
            given.append(arg)
        else:
            specs.append(VMEM)
            given.append(pltpu.with_memory_space_constraint(arg, pltpu.VMEM))
    return pl.pallas_call(
        body,
        out_shape=[pltpu.VMEM(shape, dtype) for shape, dtype in outs],
        in_specs=specs,
        out_specs=[VMEM] * len(outs),
        scratch_shapes=list(scratch),
        compiler_params=PARAMS,
        name=name,
    )(*given)


SLAB, FACE = (ROWS, COLS, DEPTH), (4, COLS, DEPTH)


def ring_of(ids):
    return ids[1] & 3, ids[1] >> 2


def serves_upper(start, ids):
    ring, upper = ring_of(ids)
    first = start >> 6
    return ((first + ((ring - first) & 3)) >> 2) == upper


def select_kernel(ids, begin, s1, s2, s3, vel, dens, other_vel, other_dens, *outs):
    for out, start in zip(outs, (begin, s3, s2, s1)):
        mine = serves_upper(start[0], ids)

        @pl.when(mine)
        def _():
            out[0] = vel[...]
            out[1] = dens[...]

        @pl.when(jnp.logical_not(mine))
        def _():
            out[0] = other_vel[...]
            out[1] = other_dens[...]


def window_pick(ids, begin):
    ring, _ = ring_of(ids)
    first, offset = begin[0] >> 6, begin[0] & 63
    want = lax.broadcasted_iota(jnp.int32, (COLS, TILE), 0) + offset
    within = lax.broadcasted_iota(jnp.int32, (COLS, TILE), 1)
    picks = [jnp.where(within + ((ring - s - first) & 3) * TILE == want, 1.0, 0.0) for s in range(4)]
    return jnp.concatenate(picks, axis=1).astype(BF16)


def window_dens_kernel(ids, begin, t0, t1, t2, t3, dens_out, core_out, cross_out, wide):
    parity = ids[0] & 1
    pick = window_pick(ids, begin)
    for s, tile in enumerate((t0, t1, t2, t3)):
        wide[:, s * TILE : (s + 1) * TILE, :] = tile[1]
    for r in range(ROWS):
        dens_out[r] = jnp.dot(pick, wide[r], preferred_element_type=F32)
    core_out[...] = dens_out[pl.ds(pl.multiple_of((1 - parity) * 4, 4), 4)].astype(BF16)
    cross_out[...] = dens_out[pl.ds(pl.multiple_of(parity * 4, 4), 4)].astype(BF16)


def coef_kernel(ids, begin, t0, t1, t2, t3, dens, depth_w, cols_w, coef, s1, s2, logs, wide):
    pick = window_pick(ids, begin)
    for s, tile in enumerate((t0, t1, t2, t3)):
        wide[:, s * TILE : (s + 1) * TILE, :] = tile[0]
    for r in range(ROWS):
        speed = jnp.dot(pick, wide[r], preferred_element_type=F32)
        c = speed * speed
        coef[r] = c * LAP_SCALE
        log = jnp.log(dens[r])
        logs[r] = log
        high, low = halves(log)
        cs = c * (SLOPE_SCALE * SLOPE_SCALE)
        s1[r] = cs * (
            jnp.dot(cols_w[COLS:], high, preferred_element_type=F32)
            + jnp.dot(cols_w[COLS:], low, preferred_element_type=F32)
        )
        s2[r] = cs * (
            jnp.dot(high, depth_w[:, DEPTH:], preferred_element_type=F32)
            + jnp.dot(low, depth_w[:, DEPTH:], preferred_element_type=F32)
        )


def row_slope_kernel(ids, logs, core, cross, coef, s0, ext):
    parity, place = ids[0] & 1, ids[0]
    pad = jnp.where((place == 0) | (place == 15), 1.0, 0.0).astype(F32)
    load_extended(ext, logs, parity, jnp.log(core[...].astype(F32)), jnp.log(cross[...].astype(F32) + pad))

    def body(i, carry):
        at = pl.ds(pl.multiple_of(i * 8, 8), 8)
        e = [ext[r, at, :] for r in range(16)]
        for r in range(ROWS):
            d0 = SLOPE[0] * (e[r + 5] - e[r + 3])
            for k in range(2, 5):
                d0 += SLOPE[k - 1] * (e[r + 4 + k] - e[r + 4 - k])
            s0[r, at, :] = (coef[r, at, :] * (SLOPE_SCALE * SLOPE_SCALE / LAP_SCALE)) * d0
        return carry

    lax.fori_loop(0, COLS // 8, body, 0)


def step_kernel(mode, first, moment, *refs):
    refs = list(refs)
    ids = refs.pop(0)
    cell, amount = (refs.pop(0), refs.pop(0)) if mode == "fwd" else (None, None)
    prev, now, core, cross = refs[:4]
    refs = refs[4:]
    if first:
        qs_now = None
    else:
        qr_now, qr_prev, qs_now, qs_prev = refs[:4]
        refs = refs[4:]
    plane = refs.pop(0) if mode == "bwd" else None
    coef, s0, s1, s2, depth_w, cols_w = refs[:6]
    refs = refs[6:]
    out = refs.pop(0)
    last = len(refs) == 3
    if not last:
        core_out, cross_out, qr_out, qs_out = refs[:4]
        refs = refs[4:]
    ext, zz, cc = refs
    parity = ids[0] & 1
    if first:
        seen = cross[...]
    else:
        seen = (2.0 * qr_now[...] - qr_prev[...]) + cross[...].astype(F32)
    load_extended(ext, now, parity, core[...], seen)
    if not last:
        qr_out[...] = seen
    in_plane(ext, depth_w, cols_w, zz, cc)

    def body(i, carry):
        at = pl.ds(pl.multiple_of(i * 8, 8), 8)
        at2 = pl.ds(pl.multiple_of(COLS + i * 8, 8), 8)
        e = [ext[r, at, :] for r in range(16)]
        for r in range(ROWS):
            mid = e[r + 4]
            lap = (3.0 * LAP[0]) * mid + (cc[r, at, :] + zz[r, at, :DEPTH])
            d0 = None
            for k in range(1, 5):
                hi, lo = e[r + 4 + k], e[r + 4 - k]
                lap += LAP[k] * (hi + lo)
                term = SLOPE[k - 1] * (hi - lo)
                d0 = term if d0 is None else d0 + term
            drift = s0[r, at, :] * d0 + s1[r, at, :] * cc[r, at2, :] + s2[r, at, :] * zz[r, at, DEPTH:]
            new = 2.0 * mid - prev[r, at, :] + (coef[r, at, :] * lap - drift)
            if mode == "bwd":
                out[r, at, :128] = new[:, :128] + plane[moment, r, at, :]
                out[r, at, 128:] = new[:, 128:]
            else:
                out[r, at, :] = new
        return carry

    lax.fori_loop(0, COLS // 8, body, 0)

    if mode == "fwd":

        line = cell[0] >> 8
        row = lax.div(line, COLS) - ids[0] * ROWS

        @pl.when((row >= 0) & (row < ROWS))
        def _():
            col = lax.rem(line, COLS)
            base = pl.multiple_of(col & ~7, 8)
            col_in = lax.broadcasted_iota(jnp.int32, (8, DEPTH), 0)
            depth_in = lax.broadcasted_iota(jnp.int32, (8, DEPTH), 1)
            struck = (col_in == (col & 7)) & (depth_in == (cell[0] & 255))
            out[row, pl.ds(base, 8), :] += jnp.where(struck, amount[moment], 0.0)

    if not last:
        core_out[...] = out[pl.ds(pl.multiple_of((1 - parity) * 4, 4), 4)]
        rows = out[pl.ds(pl.multiple_of(parity * 4, 4), 4)]
        if first:
            own = now[pl.ds(pl.multiple_of(parity * 4, 4), 4)]
            base = own
        else:
            base = 2.0 * qs_now[...] - qs_prev[...]
        sent = (rows - base).astype(BF16)
        cross_out[...] = sent
        qs_out[...] = base + sent.astype(F32)


def step(mode, moment, ids, source, prev, now, core, cross, quant, planes, fields, tables):
    first, last = moment == 0, moment == STEPS - 1
    args = [ids]
    if mode == "fwd":
        args += list(source)
    args += [prev, now, core, cross]
    if not first:
        args += list(quant)
    if mode == "bwd":
        args.append(planes)
    args += list(fields) + list(tables)
    outs = [(SLAB, F32)]
    if not last:
        outs += [(FACE, F32), (FACE, BF16), (FACE, F32), (FACE, F32)]
    scratch = [
        pltpu.VMEM((ROWS + 8, COLS, DEPTH), F32),
        pltpu.VMEM((ROWS, COLS, 2 * DEPTH), F32),
        pltpu.VMEM((ROWS, 2 * COLS, DEPTH), F32),
    ]
    return call(functools.partial(step_kernel, mode, first, moment), args, outs, scratch, "step_" + mode)


def blocks_kernel(ids, begin, part, a5, s0, a0, s5, b0, b1, b2, b3):
    ring, _ = ring_of(ids)
    first, offset = begin[0] >> 6, begin[0] & 63
    within = lax.broadcasted_iota(jnp.int32, (TILE, COLS), 0)
    column = lax.broadcasted_iota(jnp.int32, (TILE, COLS), 1) + offset
    picks = [jnp.where(within + ((ring + s - first) & 3) * TILE == column, 1.0, 0.0) for s in range(4)]
    pick = jnp.concatenate(picks, axis=0).astype(BF16)
    for r in range(ROWS):
        total = part[r] + a5[r] * s0[r] + a0[r] * s5[r]
        high, low = halves(total)
        placed = jnp.dot(pick, high, preferred_element_type=F32) + jnp.dot(
            pick, low, preferred_element_type=F32
        )
        for s, block in enumerate((b0, b1, b2, b3)):
            block[r] = placed[s * TILE : (s + 1) * TILE]


def combine_kernel(ids, begin, s1, s2, s3, b0, b1, b2, b3, keep, give):
    flags = [jnp.where(serves_upper(start[0], ids), 1.0, 0.0).astype(F32) for start in (begin, s1, s2, s3)]
    for r in range(ROWS):
        kept = flags[0] * b0[r]
        total = b0[r]
        for flag, block in zip(flags[1:], (b1, b2, b3)):
            kept += flag * block[r]
            total += block[r]
        keep[r] = kept
        gave = (1.0 - flags[0]) * b0[r]
        for flag, block in zip(flags[1:], (b1, b2, b3)):
            gave += (1.0 - flag) * block[r]
        give[r] = gave


def shards(
    forward_prev,
    forward_now,
    adjoint_prev,
    adjoint_now,
    velocity,
    density,
    anchors,
    shot_cell,
    wavelet,
    records,
):
    tables = weight_tables()
    place = lax.axis_index("apert")
    shot = lax.axis_index("shot")
    count = lax.axis_size("apert")
    groups = lax.axis_size("shot")
    half = groups // 2
    parity = place & 1
    ids = jnp.stack([place, shot]).astype(jnp.int32)
    core_pairs = [(i, i ^ 1) for i in range(count)]
    cross_pairs = [(i, i + 1) for i in range(1, count - 1, 2)] + [(i + 1, i) for i in range(1, count - 1, 2)]
    side_pairs = [(i, (i + half) % groups) for i in range(groups)]

    def ring_pairs(shift):
        return [(i, (i // half) * half + (i % half + shift) % half) for i in range(groups)]

    def faces(field):
        return (
            lax.dynamic_slice_in_dim(field, (1 - parity) * 4, 4, 0),
            lax.dynamic_slice_in_dim(field, parity * 4, 4, 0),
        )

    def swap(core, cross):
        return lax.ppermute(core, "apert", core_pairs), lax.ppermute(cross, "apert", cross_pairs)

    starts = [lax.ppermute(anchors, "shot", ring_pairs(k)) for k in range(1, half)]
    other_vel = lax.ppermute(velocity, "shot", side_pairs)
    other_dens = lax.ppermute(density, "shot", side_pairs)
    tile2 = ((2, ROWS, TILE, DEPTH), BF16)
    tiles = call(
        select_kernel, [ids, anchors, *starts, velocity, density, other_vel, other_dens], [tile2] * half, name="select"
    )
    tiles = [tiles[0]] + [lax.ppermute(tiles[k], "shot", ring_pairs(k)) for k in range(1, half)]

    fwd_prev, fwd_now, bwd_prev, bwd_now = forward_prev[0], forward_now[0], adjoint_prev[0], adjoint_now[0]
    fwd_faces, bwd_faces = faces(fwd_now), faces(bwd_now)
    fwd_core, fwd_cross = swap(*fwd_faces)
    bwd_core, bwd_cross = swap(*bwd_faces)

    wide = [pltpu.VMEM((ROWS, 4 * TILE, DEPTH), BF16)]
    dens, dens_core, dens_cross = call(
        window_dens_kernel, [ids, anchors, *tiles], [(SLAB, F32), (FACE, BF16), (FACE, BF16)], wide, "window_dens"
    )
    dens_core, dens_cross = swap(dens_core, dens_cross)
    coef, slope1, slope2, logs = call(
        coef_kernel, [ids, anchors, *tiles, dens, *tables], [(SLAB, F32)] * 4, wide, "coef"
    )
    (slope0,) = call(
        row_slope_kernel,
        [ids, logs, dens_core, dens_cross, coef],
        [(SLAB, F32)],
        [pltpu.VMEM((ROWS + 8, COLS, DEPTH), F32)],
        "row_slope",
    )
    fields = (coef, slope0, slope1, slope2)
    lane = lax.broadcasted_iota(jnp.int32, (1, 1, 1, 128), 3)
    planes = jnp.where(lane == SURF, records[0][..., None], 0.0)
    source = (shot_cell, wavelet[0])

    fwd_quant = bwd_quant = None
    snapshots, states = [], []
    for moment in range(STEPS):
        last = moment == STEPS - 1
        if moment > 0:
            fwd_core, fwd_cross = swap(fwd_core, fwd_cross)
        new, *sent = step(
            "fwd", moment, ids, source, fwd_prev, fwd_now, fwd_core, fwd_cross, fwd_quant, None, fields, tables
        )
        if not last:
            own = fwd_faces[1] if moment == 0 else fwd_quant[2]
            fwd_core, fwd_cross, seen, shown = sent
            fwd_quant = (seen, seen if moment == 0 else fwd_quant[0], shown, own)
        snapshots.append(new)
        fwd_prev, fwd_now = fwd_now, new

        if moment > 0:
            bwd_core, bwd_cross = swap(bwd_core, bwd_cross)
        new, *sent = step(
            "bwd", moment, ids, source, bwd_prev, bwd_now, bwd_core, bwd_cross, bwd_quant, planes, fields, tables
        )
        if not last:
            own = bwd_faces[1] if moment == 0 else bwd_quant[2]
            bwd_core, bwd_cross, seen, shown = sent
            bwd_quant = (seen, seen if moment == 0 else bwd_quant[0], shown, own)
        states.append(new)
        bwd_prev, bwd_now = bwd_now, new
    part = sum(states[t] * snapshots[STEPS - 1 - t] for t in range(1, STEPS - 1))

    block = ((ROWS, TILE, DEPTH), F32)
    blocks = call(
        blocks_kernel,
        [ids, anchors, part, states[STEPS - 1], snapshots[0], states[0], snapshots[STEPS - 1]],
        [block] * half,
        name="blocks",
    )
    arrived = [blocks[0]] + [lax.ppermute(blocks[k], "shot", ring_pairs(k)) for k in range(1, half)]
    keep, give = call(combine_kernel, [ids, anchors, *starts, *arrived], [block] * 2, name="combine")
    image = keep + lax.ppermute(give, "shot", side_pairs)
    return image, states[STEPS - 1][None]


def solution(mesh):
    placed = (
        P("shot", "apert", None, None),
        P("shot", "apert", None, None),
        P("shot", "apert", None, None),
        P("shot", "apert", None, None),
        P("apert", "shot", None),
        P("apert", "shot", None),
        P("shot"),
        P("shot"),
        P("shot", None),
        P("shot", None, "apert", None),
    )
    return jax.shard_map(
        shards,
        mesh=mesh,
        in_specs=placed,
        out_specs=(P("apert", "shot", None), P("shot", "apert", None, None)),
        check_vma=False,
    )
```

time: 349 us -> 270 us (0.77)
  Pallas kernels: 150 us -> 79.5 us
  waiting for transfers between devices: 58 us -> 102 us
  between operations: 20.8 us -> 2.41 us
  local copies, waits for them, and re-layouts: 20.1 us -> 4.54 us
  blocking collectives: 9.69 us -> 0 us
  other arithmetic: 11.5 us -> 2.73 us
    pallas_call x15 -> x18, Pallas kernels: 150 us -> 79.5 us  [call(): pl.pallas_call(body, out_shape=[pltpu.VMEM(shape, dtype) for shape, dtype...]
    ppermute x13, waiting for transfers between devices: 25.1 us -> 51.9 us  [swap(): lax.ppermute(cross, 'apert', cross_pairs)]
    ppermute x7 -> x11, waiting for transfers between devices: 21 us -> 37.9 us  [the longest x3 20.1 us: shards(): lax.ppermute(blocks[k], 'shot', ring_pairs(k))]
    unnamed x85 -> x21, local copies, waits for them, and re-layouts: 13 us -> 3.09 us
    unnamed x1 -> x0, blocking collectives: 9.69 us -> none
    ppermute x13, starting transfers between devices: 16.2 us -> 6.52 us  [swap(): lax.ppermute(core, 'apert', core_pairs)]
    ppermute x7 -> x11, starting transfers between devices: 7.08 us -> 16.3 us  [the longest x3 5.59 us: shards(): lax.ppermute(anchors, 'shot', ring_pairs(k))]
  transfers between devices with their start and end apart: 34 -> 38, of which waited for: 10 -> 20; matrix products, arithmetic and copies ran while one was open for 5% -> 2% of each run, Pallas kernels for 39% -> 25%
where the time goes in v2:
time: 270 us; the launch traced here: 267 us
  waiting for transfers between devices  102 us (38%)
  Pallas kernels  79.5 us (29%)
  starting transfers between devices  75.7 us (28%)
  local copies, waits for them, and re-layouts  4.54 us (2%)
  other arithmetic  2.73 us (1%)
    pallas_call x18, Pallas kernels, call(): pl.pallas_call(body, out_shape=[pltpu.VMEM(shape, dtype) for shape, dtype...  79.5 us
    ppermute x13, starting transfers between devices, swap(): lax.ppermute(cross, 'apert', cross_pairs)  52.2 us
    ppermute x13, waiting for transfers between devices, swap(): lax.ppermute(cross, 'apert', cross_pairs)  51.9 us
    ppermute x3, waiting for transfers between devices, shards(): lax.ppermute(blocks[k], 'shot', ring_pairs(k))  20.1 us
    ppermute x3, waiting for transfers between devices, shards(): lax.ppermute(tiles[k], 'shot', ring_pairs(k))  12.6 us
    ppermute x1, waiting for transfers between devices, shards(): image = keep + lax.ppermute(give, 'shot', side_pairs)  12.3 us
    ppermute x13, starting transfers between devices, swap(): lax.ppermute(core, 'apert', core_pairs)  6.52 us
    ppermute x3, starting transfers between devices, shards(): lax.ppermute(anchors, 'shot', ring_pairs(k))  5.59 us
  transfers between devices with their start and end apart: 38, of which 20 were waited for; matrix products, arithmetic and copies ran while one was open for 2% of the time, Pallas kernels for 25%

profile of v2, /device:TPU:7, one launch (start us, length us, event | category | flops | bytes accessed | tf_op | source)
XLA Modules:
  0.0 267.0 jit_solution(2228873368512638428)
XLA Ops:
  32.3 12.4 %collective-permute-done.8.t2 = bf16[2,8,64,256]{3,2,1,0:T(8,128)(2,1)S(1)} collective-permute-done((bf16[2,8,64,256]{3,2,1,0:T(8,128)(2,1)S(1)}, bf16[2,8,64,256]{3,2,1,0:T(8,128)(2,1)S(1)}, u32[]{:S(2)}, u32[]{:S(2)}) %collective-permute-start.8) | collective-permute-done | bytes 524320 | tf_op jit(solution)/shard_map/ppermute | solution.py:354
  60.0 16.6 %collective-permute-done.11.cross = bf16[4,160,256]{2,1,0:T(8,128)(2,1)S(1)} collective-permute-done((bf16[4,160,256]{2,1,0:T(8,128)(2,1)S(1)}, bf16[4,160,256]{2,1,0:T(8,128)(2,1)S(1)}, u32[]{:S(2)}, u32[]{:S(2)}) %collective-permute-start.11) | collective-permute-done | bytes 327712 | tf_op jit(solution)/shard_map/ppermute | solution.py:345
  78.4 5.6 %step_fwd.6 = (f32[8,160,256]{2,1,0:T(8,128)S(1)}, f32[4,160,256]{2,1,0:T(8,128)S(1)}, bf16[4,160,256]{2,1,0:T(8,128)(2,1)S(1)}, f32[4,160,256]{2,1,0:T(8,128)S(1)}, f32[4,160,256]{2,1,0:T(8,128)S(1)}) custom-call(s32[2]{0:T(128)S(1)} %pad_add_fusion.ids.refs_0_, s32[1]{0:T(128)S(6)} %copy.16.refs_1_, f32[6]{0:T(128)S(1)} %bitcast.24, ...), custom_call_target="tpu_custom_call" | custom-call | tf_op jit(solution)/shard_map/step_fwd/pallas_call | solution.py:77
  84.1 5.7 %step_bwd.6 = (f32[8,160,256]{2,1,0:T(8,128)S(1)}, f32[4,160,256]{2,1,0:T(8,128)S(1)}, bf16[4,160,256]{2,1,0:T(8,128)(2,1)S(1)}, f32[4,160,256]{2,1,0:T(8,128)S(1)}, f32[4,160,256]{2,1,0:T(8,128)S(1)}) custom-call(s32[2]{0:T(128)S(1)} %pad_add_fusion.ids.refs_0_, f32[8,160,256]{2,1,0:T(8,128)S(1)} %bitcast.23, f32[8,160,256]{2,1,0:T(8,128)S(1)} %bitcast.20, ...), custom_call_target="tpu_custom_call" | custom-call | tf_op jit(solution)/shard_map/step_bwd/pallas_call | solution.py:77
  98.3 6.3 %collective-permute-done.17.refs_6_ = bf16[4,160,256]{2,1,0:T(8,128)(2,1)S(1)} collective-permute-done((bf16[4,160,256]{2,1,0:T(8,128)(2,1)S(1)}, bf16[4,160,256]{2,1,0:T(8,128)(2,1)S(1)}, u32[]{:S(2)}, u32[]{:S(2)}) %collective-permute-start.17) | collective-permute-done | bytes 327712 | tf_op jit(solution)/shard_map/ppermute | solution.py:345
  104.6 5.7 %step_fwd.7 = (f32[8,160,256]{2,1,0:T(8,128)S(1)}, f32[4,160,256]{2,1,0:T(8,128)S(1)}, bf16[4,160,256]{2,1,0:T(8,128)(2,1)S(1)}, f32[4,160,256]{2,1,0:T(8,128)S(1)}, f32[4,160,256]{2,1,0:T(8,128)S(1)}) custom-call(s32[2]{0:T(128)S(1)} %pad_add_fusion.ids.refs_0_, s32[1]{0:T(128)S(6)} %copy.16.refs_1_, f32[6]{0:T(128)S(1)} %bitcast.25, ...), custom_call_target="tpu_custom_call" | custom-call | tf_op jit(solution)/shard_map/step_fwd/pallas_call | solution.py:77
  111.4 5.7 %step_bwd.7 = (f32[8,160,256]{2,1,0:T(8,128)S(1)}, f32[4,160,256]{2,1,0:T(8,128)S(1)}, bf16[4,160,256]{2,1,0:T(8,128)(2,1)S(1)}, f32[4,160,256]{2,1,0:T(8,128)S(1)}, f32[4,160,256]{2,1,0:T(8,128)S(1)}) custom-call(s32[2]{0:T(128)S(1)} %pad_add_fusion.ids.refs_0_, f32[8,160,256]{2,1,0:T(8,128)S(1)} %bitcast.21, ...), custom_call_target="tpu_custom_call" | custom-call | tf_op jit(solution)/shard_map/step_bwd/pallas_call | solution.py:77
  125.4 6.0 %collective-permute-done.19.refs_6_ = bf16[4,160,256]{2,1,0:T(8,128)(2,1)S(1)} collective-permute-done((bf16[4,160,256]{2,1,0:T(8,128)(2,1)S(1)}, bf16[4,160,256]{2,1,0:T(8,128)(2,1)S(1)}, u32[]{:S(2)}, u32[]{:S(2)}) %collective-permute-start.19) | collective-permute-done | bytes 327712 | tf_op jit(solution)/shard_map/ppermute | solution.py:345
  131.4 5.7 %step_fwd.8 = (f32[8,160,256]{2,1,0:T(8,128)S(1)}, f32[4,160,256]{2,1,0:T(8,128)S(1)}, bf16[4,160,256]{2,1,0:T(8,128)(2,1)S(1)}, f32[4,160,256]{2,1,0:T(8,128)S(1)}, f32[4,160,256]{2,1,0:T(8,128)S(1)}) custom-call(s32[2]{0:T(128)S(1)} %pad_add_fusion.ids.refs_0_, s32[1]{0:T(128)S(6)} %copy.16.refs_1_, f32[6]{0:T(128)S(1)} %bitcast.26, ...), custom_call_target="tpu_custom_call" | custom-call | tf_op jit(solution)/shard_map/step_fwd/pallas_call | solution.py:77
  138.4 5.7 %step_bwd.8 = (f32[8,160,256]{2,1,0:T(8,128)S(1)}, f32[4,160,256]{2,1,0:T(8,128)S(1)}, bf16[4,160,256]{2,1,0:T(8,128)(2,1)S(1)}, f32[4,160,256]{2,1,0:T(8,128)S(1)}, f32[4,160,256]{2,1,0:T(8,128)S(1)}) custom-call(s32[2]{0:T(128)S(1)} %pad_add_fusion.ids.refs_0_, f32[8,160,256]{2,1,0:T(8,128)S(1)} %get-tuple-element.80.refs_2_.refs_1_.a0, ...), custom_call_target="tpu_custom_call" | custom-call | tf_op jit(solution)/shard_map/step_bwd/pallas_call | solution.py:77
  152.2 6.0 %collective-permute-done.21.refs_6_ = bf16[4,160,256]{2,1,0:T(8,128)(2,1)S(1)} collective-permute-done((bf16[4,160,256]{2,1,0:T(8,128)(2,1)S(1)}, bf16[4,160,256]{2,1,0:T(8,128)(2,1)S(1)}, u32[]{:S(2)}, u32[]{:S(2)}) %collective-permute-start.21) | collective-permute-done | bytes 327712 | tf_op jit(solution)/shard_map/ppermute | solution.py:345
  158.2 5.7 %step_fwd.9 = (f32[8,160,256]{2,1,0:T(8,128)S(1)}, f32[4,160,256]{2,1,0:T(8,128)S(1)}, bf16[4,160,256]{2,1,0:T(8,128)(2,1)S(1)}, f32[4,160,256]{2,1,0:T(8,128)S(1)}, f32[4,160,256]{2,1,0:T(8,128)S(1)}) custom-call(s32[2]{0:T(128)S(1)} %pad_add_fusion.ids.refs_0_, s32[1]{0:T(128)S(6)} %copy.16.refs_1_, f32[6]{0:T(128)S(1)} %bitcast.27, ...), custom_call_target="tpu_custom_call" | custom-call | tf_op jit(solution)/shard_map/step_fwd/pallas_call | solution.py:77
  165.2 5.7 %step_bwd.9 = (f32[8,160,256]{2,1,0:T(8,128)S(1)}, f32[4,160,256]{2,1,0:T(8,128)S(1)}, bf16[4,160,256]{2,1,0:T(8,128)(2,1)S(1)}, f32[4,160,256]{2,1,0:T(8,128)S(1)}, f32[4,160,256]{2,1,0:T(8,128)S(1)}) custom-call(s32[2]{0:T(128)S(1)} %pad_add_fusion.ids.refs_0_, f32[8,160,256]{2,1,0:T(8,128)S(1)} %get-tuple-element.85.refs_2_.refs_1_, ...), custom_call_target="tpu_custom_call" | custom-call | tf_op jit(solution)/shard_map/step_bwd/pallas_call | solution.py:77
  174.0 5.0 %collective-permute-start.29 = (bf16[4,160,256]{2,1,0:T(8,128)(2,1)S(1)}, bf16[4,160,256]{2,1,0:T(8,128)(2,1)S(1)}, u32[]{:S(2)}, u32[]{:S(2)}) collective-permute-start(bf16[4,160,256]{2,1,0:T(8,128)(2,1)S(1)} %get-tuple-element.118), channel_id=1, source_target_pairs={{1,2},{3,4},{5,6},{7,8},{9,10},{11,12},{13,14},{2,1},{4,3},{6,5},{... | collective-permute-start | bytes 983048 | tf_op jit(solution)/shard_map/ppermute | solution.py:345
  179.0 6.2 %collective-permute-done.23.refs_6_ = bf16[4,160,256]{2,1,0:T(8,128)(2,1)S(1)} collective-permute-done((bf16[4,160,256]{2,1,0:T(8,128)(2,1)S(1)}, bf16[4,160,256]{2,1,0:T(8,128)(2,1)S(1)}, u32[]{:S(2)}, u32[]{:S(2)}) %collective-permute-start.23) | collective-permute-done | bytes 327712 | tf_op jit(solution)/shard_map/ppermute | solution.py:345
  185.3 5.7 %step_fwd.10 = (f32[8,160,256]{2,1,0:T(8,128)S(1)}, f32[4,160,256]{2,1,0:T(8,128)S(1)}, bf16[4,160,256]{2,1,0:T(8,128)(2,1)S(1)}, f32[4,160,256]{2,1,0:T(8,128)S(1)}, f32[4,160,256]{2,1,0:T(8,128)S(1)}) custom-call(s32[2]{0:T(128)S(1)} %pad_add_fusion.ids.refs_0_, s32[1]{0:T(128)S(6)} %copy.16.refs_1_, f32[6]{0:T(128)S(1)} %bitcast.28, ...), custom_call_target="tpu_custom_call" | custom-call | tf_op jit(solution)/shard_map/step_fwd/pallas_call | solution.py:77
  192.0 5.8 %step_bwd.10 = (f32[8,160,256]{2,1,0:T(8,128)S(1)}, f32[4,160,256]{2,1,0:T(8,128)S(1)}, bf16[4,160,256]{2,1,0:T(8,128)(2,1)S(1)}, f32[4,160,256]{2,1,0:T(8,128)S(1)}, f32[4,160,256]{2,1,0:T(8,128)S(1)}) custom-call(s32[2]{0:T(128)S(1)} %pad_add_fusion.ids.refs_0_, f32[8,160,256]{2,1,0:T(8,128)S(1)} %get-tuple-element.111.refs_2_.refs_1_, ...), custom_call_target="tpu_custom_call" | custom-call | tf_op jit(solution)/shard_map/step_bwd/pallas_call | solution.py:77
  200.9 5.0 %collective-permute-start.31 = (bf16[4,160,256]{2,1,0:T(8,128)(2,1)S(1)}, bf16[4,160,256]{2,1,0:T(8,128)(2,1)S(1)}, u32[]{:S(2)}, u32[]{:S(2)}) collective-permute-start(bf16[4,160,256]{2,1,0:T(8,128)(2,1)S(1)} %get-tuple-element.123), channel_id=1, source_target_pairs={{1,2},{3,4},{5,6},{7,8},{9,10},{11,12},{13,14},{2,1},{4,3},{6,5},{... | collective-permute-start | bytes 983048 | tf_op jit(solution)/shard_map/ppermute | solution.py:345
  206.6 5.6 %collective-permute-done.33.refs_6_ = bf16[4,160,256]{2,1,0:T(8,128)(2,1)S(1)} collective-permute-done((bf16[4,160,256]{2,1,0:T(8,128)(2,1)S(1)}, bf16[4,160,256]{2,1,0:T(8,128)(2,1)S(1)}, u32[]{:S(2)}, u32[]{:S(2)}) %collective-permute-start.33) | collective-permute-done | bytes 327712 | tf_op jit(solution)/shard_map/ppermute | solution.py:345
  212.2 5.4 %step_fwd.11.s5 = f32[8,160,256]{2,1,0:T(8,128)S(1)} custom-call(s32[2]{0:T(128)S(1)} %pad_add_fusion.ids.refs_0_, s32[1]{0:T(128)S(6)} %copy.16.refs_1_, f32[6]{0:T(128)S(1)} %bitcast.29, f32[8,160,256]{2,1,0:T(8,128)S(1)} %get-tuple-element.101.refs_4_.refs_3_, f32[8,160,256]{2,1,0:T(8,128)S(1)} %get-tuple-element.106.refs_4_, ...), custom_call_target="tpu_custom_call" | custom-call | tf_op jit(solution)/shard_map/step_fwd/pallas_call | solution.py:77
  218.3 5.5 %step_bwd.11.a5 = f32[8,160,256]{2,1,0:T(8,128)S(1)} custom-call(s32[2]{0:T(128)S(1)} %pad_add_fusion.ids.refs_0_, f32[8,160,256]{2,1,0:T(8,128)S(1)} %get-tuple-element.116.refs_2_.refs_1_, f32[8,160,256]{2,1,0:T(8,128)S(1)} %get-tuple-element.121.refs_2_, f32[4,160,256]{2,1,0:T(8,128)S(1)} %collective-permute-done.30.refs_3_, ...), custom_call_target="tpu_custom_call" | custom-call | tf_op jit(solution)/shard_map/step_bwd/pallas_call | solution.py:77
  229.4 10.9 %collective-permute-done.34.b1 = f32[8,64,256]{2,1,0:T(8,128)S(1)} collective-permute-done((f32[8,64,256]{2,1,0:T(8,128)S(1)}, f32[8,64,256]{2,1,0:T(8,128)S(1)}, u32[]{:S(2)}, u32[]{:S(2)}) %collective-permute-start.34) | collective-permute-done | bytes 524320 | tf_op jit(solution)/shard_map/ppermute | solution.py:417
  240.3 8.4 %collective-permute-done.35.b2 = f32[8,64,256]{2,1,0:T(8,128)S(1)} collective-permute-done((f32[8,64,256]{2,1,0:T(8,128)S(1)}, f32[8,64,256]{2,1,0:T(8,128)S(1)}, u32[]{:S(2)}, u32[]{:S(2)}) %collective-permute-start.35) | collective-permute-done | bytes 524320 | tf_op jit(solution)/shard_map/ppermute | solution.py:417
  253.9 12.3 %collective-permute-done.37 = f32[8,64,256]{2,1,0:T(8,128)S(1)} collective-permute-done((f32[8,64,256]{2,1,0:T(8,128)S(1)}, f32[8,64,256]{2,1,0:T(8,128)S(1)}, u32[]{:S(2)}, u32[]{:S(2)}) %collective-permute-start.37) | collective-permute-done | bytes 524320 | tf_op jit(solution)/shard_map/ppermute | solution.py:419
  (98 shorter events, 96.0 us)
Async XLA Ops:
  20.2 24.4 %collective-permute-start.8 = (bf16[2,8,64,256]{3,2,1,0:T(8,128)(2,1)S(1)}, bf16[2,8,64,256]{3,2,1,0:T(8,128)(2,1)S(1)}, u32[]{:S(2)}, u32[]{:S(2)}) collective-permute-start(bf16[2,8,64,256]{3,2,1,0:T(8,128)(2,1)S(1)} %get-tuple-element.71), channel_id=1, source_target_pairs={{0,32},{16,48},{32,0},{48,16},{64,96},{80,112},{96,64},{112,80},{1... | collective-permute-start | bytes 1572872 | tf_op jit(solution)/shard_map/ppermute | solution.py:354
  22.8 22.0 %collective-permute-start.9 = (bf16[2,8,64,256]{3,2,1,0:T(8,128)(2,1)S(1)}, bf16[2,8,64,256]{3,2,1,0:T(8,128)(2,1)S(1)}, u32[]{:S(2)}, u32[]{:S(2)}) collective-permute-start(bf16[2,8,64,256]{3,2,1,0:T(8,128)(2,1)S(1)} %get-tuple-element.72), channel_id=1, source_target_pairs={{0,48},{16,0},{32,16},{48,32},{64,112},{80,64},{96,80},{112,96},{1... | collective-permute-start | bytes 1572872 | tf_op jit(solution)/shard_map/ppermute | solution.py:354
  25.3 52.9 %collective-permute-start.14 = (f32[4,160,256]{2,1,0:T(8,128)S(1)}, f32[4,160,256]{2,1,0:T(8,128)S(1)}, u32[]{:S(2)}, u32[]{:S(2)}) collective-permute-start(f32[4,160,256]{2,1,0:T(8,128)S(1)} %get-tuple-element.137), channel_id=1, source_target_pairs={{0,1},{1,0},{2,3},{3,2},{4,5},{5,4},{6,7},{7,6},{8,9},{9,8},{10,11... | collective-permute-start | bytes 1966088 | tf_op jit(solution)/shard_map/ppermute | solution.py:345
  27.8 50.4 %collective-permute-start.15 = (f32[4,160,256]{2,1,0:T(8,128)S(1)}, f32[4,160,256]{2,1,0:T(8,128)S(1)}, u32[]{:S(2)}, u32[]{:S(2)}) collective-permute-start(f32[4,160,256]{2,1,0:T(8,128)S(1)} %get-tuple-element.136.refs_10_), channel_id=1, source_target_pairs={{1,2},{3,4},{5,6},{7,8},{9,10},{11,12},{13,14},{2,1},{4,3},{6,5},{... | collective-permute-start | bytes 1966088 | tf_op jit(solution)/shard_map/ppermute | solution.py:345
  48.4 35.6 %collective-permute-start.3 = (f32[4,160,256]{2,1,0:T(8,128)S(1)}, f32[4,160,256]{2,1,0:T(8,128)S(1)}, u32[]{:S(2)}, u32[]{:S(2)}) collective-permute-start(f32[4,160,256]{2,1,0:T(8,128)S(1)} %get-tuple-element.139), channel_id=1, source_target_pairs={{0,1},{1,0},{2,3},{3,2},{4,5},{5,4},{6,7},{7,6},{8,9},{9,8},{10,11... | collective-permute-start | bytes 1966088 | tf_op jit(solution)/shard_map/ppermute | solution.py:345
  48.5 35.5 %collective-permute-start.4 = (f32[4,160,256]{2,1,0:T(8,128)S(1)}, f32[4,160,256]{2,1,0:T(8,128)S(1)}, u32[]{:S(2)}, u32[]{:S(2)}) collective-permute-start(f32[4,160,256]{2,1,0:T(8,128)S(1)} %get-tuple-element.138.refs_8_), channel_id=1, source_target_pairs={{1,2},{3,4},{5,6},{7,8},{9,10},{11,12},{13,14},{2,1},{4,3},{6,5},{... | collective-permute-start | bytes 1966088 | tf_op jit(solution)/shard_map/ppermute | solution.py:345
  53.3 23.3 %collective-permute-start.11 = (bf16[4,160,256]{2,1,0:T(8,128)(2,1)S(1)}, bf16[4,160,256]{2,1,0:T(8,128)(2,1)S(1)}, u32[]{:S(2)}, u32[]{:S(2)}) collective-permute-start(bf16[4,160,256]{2,1,0:T(8,128)(2,1)S(1)} %get-tuple-element.77), channel_id=1, source_target_pairs={{1,2},{3,4},{5,6},{7,8},{9,10},{11,12},{13,14},{2,1},{4,3},{6,5},{... | collective-permute-start | bytes 983048 | tf_op jit(solution)/shard_map/ppermute | solution.py:345
  83.9 20.6 %collective-permute-start.16 = (f32[4,160,256]{2,1,0:T(8,128)S(1)}, f32[4,160,256]{2,1,0:T(8,128)S(1)}, u32[]{:S(2)}, u32[]{:S(2)}) collective-permute-start(f32[4,160,256]{2,1,0:T(8,128)S(1)} %get-tuple-element.87), channel_id=1, source_target_pairs={{0,1},{1,0},{2,3},{3,2},{4,5},{5,4},{6,7},{7,6},{8,9},{9,8},{10,11... | collective-permute-start | bytes 1966088 | tf_op jit(solution)/shard_map/ppermute | solution.py:345
  89.7 21.7 %collective-permute-start.12 = (f32[4,160,256]{2,1,0:T(8,128)S(1)}, f32[4,160,256]{2,1,0:T(8,128)S(1)}, u32[]{:S(2)}, u32[]{:S(2)}) collective-permute-start(f32[4,160,256]{2,1,0:T(8,128)S(1)} %get-tuple-element.81), channel_id=1, source_target_pairs={{0,1},{1,0},{2,3},{3,2},{4,5},{5,4},{6,7},{7,6},{8,9},{9,8},{10,11... | collective-permute-start | bytes 1966088 | tf_op jit(solution)/shard_map/ppermute | solution.py:345
  94.2 17.2 %collective-permute-start.13 = (bf16[4,160,256]{2,1,0:T(8,128)(2,1)S(1)}, bf16[4,160,256]{2,1,0:T(8,128)(2,1)S(1)}, u32[]{:S(2)}, u32[]{:S(2)}) collective-permute-start(bf16[4,160,256]{2,1,0:T(8,128)(2,1)S(1)} %get-tuple-element.82), channel_id=1, source_target_pairs={{1,2},{3,4},{5,6},{7,8},{9,10},{11,12},{13,14},{2,1},{4,3},{6,5},{... | collective-permute-start | bytes 983048 | tf_op jit(solution)/shard_map/ppermute | solution.py:345
  110.3 21.1 %collective-permute-start.18 = (f32[4,160,256]{2,1,0:T(8,128)S(1)}, f32[4,160,256]{2,1,0:T(8,128)S(1)}, u32[]{:S(2)}, u32[]{:S(2)}) collective-permute-start(f32[4,160,256]{2,1,0:T(8,128)S(1)} %get-tuple-element.92), channel_id=1, source_target_pairs={{0,1},{1,0},{2,3},{3,2},{4,5},{5,4},{6,7},{7,6},{8,9},{9,8},{10,11... | collective-permute-start | bytes 1966088 | tf_op jit(solution)/shard_map/ppermute | solution.py:345
  117.1 21.2 %collective-permute-start.24 = (f32[4,160,256]{2,1,0:T(8,128)S(1)}, f32[4,160,256]{2,1,0:T(8,128)S(1)}, u32[]{:S(2)}, u32[]{:S(2)}) collective-permute-start(f32[4,160,256]{2,1,0:T(8,128)S(1)} %get-tuple-element.107), channel_id=1, source_target_pairs={{0,1},{1,0},{2,3},{3,2},{4,5},{5,4},{6,7},{7,6},{8,9},{9,8},{10,11... | collective-permute-start | bytes 1966088 | tf_op jit(solution)/shard_map/ppermute | solution.py:345
  120.8 17.6 %collective-permute-start.25 = (bf16[4,160,256]{2,1,0:T(8,128)(2,1)S(1)}, bf16[4,160,256]{2,1,0:T(8,128)(2,1)S(1)}, u32[]{:S(2)}, u32[]{:S(2)}) collective-permute-start(bf16[4,160,256]{2,1,0:T(8,128)(2,1)S(1)} %get-tuple-element.108), channel_id=1, source_target_pairs={{1,2},{3,4},{5,6},{7,8},{9,10},{11,12},{13,14},{2,1},{4,3},{6,5},{... | collective-permute-start | bytes 983048 | tf_op jit(solution)/shard_map/ppermute | solution.py:345
  137.0 21.2 %collective-permute-start.20 = (f32[4,160,256]{2,1,0:T(8,128)S(1)}, f32[4,160,256]{2,1,0:T(8,128)S(1)}, u32[]{:S(2)}, u32[]{:S(2)}) collective-permute-start(f32[4,160,256]{2,1,0:T(8,128)S(1)} %get-tuple-element.97), channel_id=1, source_target_pairs={{0,1},{1,0},{2,3},{3,2},{4,5},{5,4},{6,7},{7,6},{8,9},{9,8},{10,11... | collective-permute-start | bytes 1966088 | tf_op jit(solution)/shard_map/ppermute | solution.py:345
  144.1 21.1 %collective-permute-start.26 = (f32[4,160,256]{2,1,0:T(8,128)S(1)}, f32[4,160,256]{2,1,0:T(8,128)S(1)}, u32[]{:S(2)}, u32[]{:S(2)}) collective-permute-start(f32[4,160,256]{2,1,0:T(8,128)S(1)} %get-tuple-element.112), channel_id=1, source_target_pairs={{0,1},{1,0},{2,3},{3,2},{4,5},{5,4},{6,7},{7,6},{8,9},{9,8},{10,11... | collective-permute-start | bytes 1966088 | tf_op jit(solution)/shard_map/ppermute | solution.py:345
  147.2 18.0 %collective-permute-start.27 = (bf16[4,160,256]{2,1,0:T(8,128)(2,1)S(1)}, bf16[4,160,256]{2,1,0:T(8,128)(2,1)S(1)}, u32[]{:S(2)}, u32[]{:S(2)}) collective-permute-start(bf16[4,160,256]{2,1,0:T(8,128)(2,1)S(1)} %get-tuple-element.113), channel_id=1, source_target_pairs={{1,2},{3,4},{5,6},{7,8},{9,10},{11,12},{13,14},{2,1},{4,3},{6,5},{... | collective-permute-start | bytes 983048 | tf_op jit(solution)/shard_map/ppermute | solution.py:345
  163.9 21.3 %collective-permute-start.22 = (f32[4,160,256]{2,1,0:T(8,128)S(1)}, f32[4,160,256]{2,1,0:T(8,128)S(1)}, u32[]{:S(2)}, u32[]{:S(2)}) collective-permute-start(f32[4,160,256]{2,1,0:T(8,128)S(1)} %get-tuple-element.102), channel_id=1, source_target_pairs={{0,1},{1,0},{2,3},{3,2},{4,5},{5,4},{6,7},{7,6},{8,9},{9,8},{10,11... | collective-permute-start | bytes 1966088 | tf_op jit(solution)/shard_map/ppermute | solution.py:345
  171.0 21.0 %collective-permute-start.28 = (f32[4,160,256]{2,1,0:T(8,128)S(1)}, f32[4,160,256]{2,1,0:T(8,128)S(1)}, u32[]{:S(2)}, u32[]{:S(2)}) collective-permute-start(f32[4,160,256]{2,1,0:T(8,128)S(1)} %get-tuple-element.117), channel_id=1, source_target_pairs={{0,1},{1,0},{2,3},{3,2},{4,5},{5,4},{6,7},{7,6},{8,9},{9,8},{10,11... | collective-permute-start | bytes 1966088 | tf_op jit(solution)/shard_map/ppermute | solution.py:345
  174.0 18.0 %collective-permute-start.29 = (bf16[4,160,256]{2,1,0:T(8,128)(2,1)S(1)}, bf16[4,160,256]{2,1,0:T(8,128)(2,1)S(1)}, u32[]{:S(2)}, u32[]{:S(2)}) collective-permute-start(bf16[4,160,256]{2,1,0:T(8,128)(2,1)S(1)} %get-tuple-element.118), channel_id=1, source_target_pairs={{1,2},{3,4},{5,6},{7,8},{9,10},{11,12},{13,14},{2,1},{4,3},{6,5},{... | collective-permute-start | bytes 983048 | tf_op jit(solution)/shard_map/ppermute | solution.py:345
  191.0 21.2 %collective-permute-start.32 = (f32[4,160,256]{2,1,0:T(8,128)S(1)}, f32[4,160,256]{2,1,0:T(8,128)S(1)}, u32[]{:S(2)}, u32[]{:S(2)}) collective-permute-start(f32[4,160,256]{2,1,0:T(8,128)S(1)} %get-tuple-element.126), channel_id=1, source_target_pairs={{0,1},{1,0},{2,3},{3,2},{4,5},{5,4},{6,7},{7,6},{8,9},{9,8},{10,11... | collective-permute-start | bytes 1966088 | tf_op jit(solution)/shard_map/ppermute | solution.py:345
  197.8 20.5 %collective-permute-start.30 = (f32[4,160,256]{2,1,0:T(8,128)S(1)}, f32[4,160,256]{2,1,0:T(8,128)S(1)}, u32[]{:S(2)}, u32[]{:S(2)}) collective-permute-start(f32[4,160,256]{2,1,0:T(8,128)S(1)} %get-tuple-element.122), channel_id=1, source_target_pairs={{0,1},{1,0},{2,3},{3,2},{4,5},{5,4},{6,7},{7,6},{8,9},{9,8},{10,11... | collective-permute-start | bytes 1966088 | tf_op jit(solution)/shard_map/ppermute | solution.py:345
  200.9 17.5 %collective-permute-start.31 = (bf16[4,160,256]{2,1,0:T(8,128)(2,1)S(1)}, bf16[4,160,256]{2,1,0:T(8,128)(2,1)S(1)}, u32[]{:S(2)}, u32[]{:S(2)}) collective-permute-start(bf16[4,160,256]{2,1,0:T(8,128)(2,1)S(1)} %get-tuple-element.123), channel_id=1, source_target_pairs={{1,2},{3,4},{5,6},{7,8},{9,10},{11,12},{13,14},{2,1},{4,3},{6,5},{... | collective-permute-start | bytes 983048 | tf_op jit(solution)/shard_map/ppermute | solution.py:345
  225.9 22.8 %collective-permute-start.35 = (f32[8,64,256]{2,1,0:T(8,128)S(1)}, f32[8,64,256]{2,1,0:T(8,128)S(1)}, u32[]{:S(2)}, u32[]{:S(2)}) collective-permute-start(f32[8,64,256]{2,1,0:T(8,128)S(1)} %get-tuple-element.132), channel_id=1, source_target_pairs={{0,32},{16,48},{32,0},{48,16},{64,96},{80,112},{96,64},{112,80},{1... | collective-permute-start | bytes 1572872 | tf_op jit(solution)/shard_map/ppermute | solution.py:417
  228.0 21.5 %collective-permute-start.36 = (f32[8,64,256]{2,1,0:T(8,128)S(1)}, f32[8,64,256]{2,1,0:T(8,128)S(1)}, u32[]{:S(2)}, u32[]{:S(2)}) collective-permute-start(f32[8,64,256]{2,1,0:T(8,128)S(1)} %get-tuple-element.133), channel_id=1, source_target_pairs={{0,48},{16,0},{32,16},{48,32},{64,112},{80,64},{96,80},{112,96},{1... | collective-permute-start | bytes 1572872 | tf_op jit(solution)/shard_map/ppermute | solution.py:417
  (24 other events, 203.7 us)

commit v3 on v2

--- a/solution.py
+++ b/solution.py
@@ -65,7 +65,7 @@
     ext[pl.ds(cross_at, 4)] = cross_rows
 
 
-def call(body, args, outs, scratch=(), name=None):
+def call(body, args, outs, scratch=(), name=None, flops=20_000_000_000):
     specs, given = [], []
     for arg in args:
         if arg.ndim == 1:
@@ -81,6 +81,7 @@
         out_specs=[VMEM] * len(outs),
         scratch_shapes=list(scratch),
         compiler_params=PARAMS,
+        cost_estimate=pl.CostEstimate(flops=flops, bytes_accessed=100_000, transcendentals=0),
         name=name,
     )(*given)
 
@@ -98,9 +99,25 @@
     return ((first + ((ring - first) & 3)) >> 2) == upper
 
 
-def select_kernel(ids, begin, s1, s2, s3, vel, dens, other_vel, other_dens, *outs):
-    for out, start in zip(outs, (begin, s3, s2, s1)):
-        mine = serves_upper(start[0], ids)
+def faces_kernel(ids, fwd, bwd, vel, dens, core, cross, own_fwd, own_bwd, vel_out, dens_out):
+    parity = ids[0] & 1
+    for f, (field, own) in enumerate(((fwd, own_fwd), (bwd, own_bwd))):
+        core[f] = field[pl.ds(pl.multiple_of((1 - parity) * 4, 4), 4)]
+        own[...] = field[pl.ds(pl.multiple_of(parity * 4, 4), 4)]
+        high = own[...].astype(BF16)
+        cross[f, :4] = high
+        near = parity * 3
+        low = (own[near] - own[near].astype(BF16).astype(F32)).astype(BF16)
+        cross[f, 4] = low
+        own[...] = high.astype(F32)
+        own[near] += low.astype(F32)
+    vel_out[...] = vel[...]
+    dens_out[...] = dens[...]
+
+
+def select_kernel(ids, vel, dens, other_vel, other_dens, *outs):
+    for out, start in zip(outs, (ids[2], ids[6], ids[5], ids[4])):
+        mine = serves_upper(start, ids)
 
         @pl.when(mine)
         def _():
@@ -113,18 +130,18 @@
             out[1] = other_dens[...]
 
 
-def window_pick(ids, begin):
+def window_pick(ids):
     ring, _ = ring_of(ids)
-    first, offset = begin[0] >> 6, begin[0] & 63
+    first, offset = ids[2] >> 6, ids[2] & 63
     want = lax.broadcasted_iota(jnp.int32, (COLS, TILE), 0) + offset
     within = lax.broadcasted_iota(jnp.int32, (COLS, TILE), 1)
     picks = [jnp.where(within + ((ring - s - first) & 3) * TILE == want, 1.0, 0.0) for s in range(4)]
     return jnp.concatenate(picks, axis=1).astype(BF16)
 
 
-def window_dens_kernel(ids, begin, t0, t1, t2, t3, dens_out, core_out, cross_out, wide):
+def window_dens_kernel(ids, t0, t1, t2, t3, dens_out, core_out, cross_out, wide):
     parity = ids[0] & 1
-    pick = window_pick(ids, begin)
+    pick = window_pick(ids)
     for s, tile in enumerate((t0, t1, t2, t3)):
         wide[:, s * TILE : (s + 1) * TILE, :] = tile[1]
     for r in range(ROWS):
@@ -133,8 +150,8 @@
     cross_out[...] = dens_out[pl.ds(pl.multiple_of(parity * 4, 4), 4)].astype(BF16)
 
 
-def coef_kernel(ids, begin, t0, t1, t2, t3, dens, depth_w, cols_w, coef, s1, s2, logs, wide):
-    pick = window_pick(ids, begin)
+def coef_kernel(ids, t0, t1, t2, t3, dens, depth_w, cols_w, coef, s1, s2, logs, wide):
+    pick = window_pick(ids)
     for s, tile in enumerate((t0, t1, t2, t3)):
         wide[:, s * TILE : (s + 1) * TILE, :] = tile[0]
     for r in range(ROWS):
@@ -176,11 +193,12 @@
 def step_kernel(mode, first, moment, *refs):
     refs = list(refs)
     ids = refs.pop(0)
-    cell, amount = (refs.pop(0), refs.pop(0)) if mode == "fwd" else (None, None)
+    amount = refs.pop(0) if mode == "fwd" else None
     prev, now, core, cross = refs[:4]
     refs = refs[4:]
+    which = 0 if mode == "fwd" else 1
     if first:
-        qs_now = None
+        own = refs.pop(0)
     else:
         qr_now, qr_prev, qs_now, qs_prev = refs[:4]
         refs = refs[4:]
@@ -195,12 +213,13 @@
     ext, zz, cc = refs
     parity = ids[0] & 1
     if first:
-        seen = cross[...]
+        load_extended(ext, now, parity, core[which], cross[which, :4].astype(F32))
+        ext[12 * parity + 3 - 3 * parity] += cross[which, 4].astype(F32)
     else:
         seen = (2.0 * qr_now[...] - qr_prev[...]) + cross[...].astype(F32)
-    load_extended(ext, now, parity, core[...], seen)
+        load_extended(ext, now, parity, core[...], seen)
     if not last:
-        qr_out[...] = seen
+        qr_out[...] = ext[pl.ds(pl.multiple_of(parity * 12, 4), 4)]
     in_plane(ext, depth_w, cols_w, zz, cc)
 
     def body(i, carry):
@@ -229,7 +248,7 @@
 
     if mode == "fwd":
 
-        line = cell[0] >> 8
+        line = ids[3] >> 8
         row = lax.div(line, COLS) - ids[0] * ROWS
 
         @pl.when((row >= 0) & (row < ROWS))
@@ -238,15 +257,14 @@
             base = pl.multiple_of(col & ~7, 8)
             col_in = lax.broadcasted_iota(jnp.int32, (8, DEPTH), 0)
             depth_in = lax.broadcasted_iota(jnp.int32, (8, DEPTH), 1)
-            struck = (col_in == (col & 7)) & (depth_in == (cell[0] & 255))
+            struck = (col_in == (col & 7)) & (depth_in == (ids[3] & 255))
             out[row, pl.ds(base, 8), :] += jnp.where(struck, amount[moment], 0.0)
 
     if not last:
         core_out[...] = out[pl.ds(pl.multiple_of((1 - parity) * 4, 4), 4)]
         rows = out[pl.ds(pl.multiple_of(parity * 4, 4), 4)]
         if first:
-            own = now[pl.ds(pl.multiple_of(parity * 4, 4), 4)]
-            base = own
+            base = own[...]
         else:
             base = 2.0 * qs_now[...] - qs_prev[...]
         sent = (rows - base).astype(BF16)
@@ -258,10 +276,8 @@
     first, last = moment == 0, moment == STEPS - 1
     args = [ids]
     if mode == "fwd":
-        args += list(source)
-    args += [prev, now, core, cross]
-    if not first:
-        args += list(quant)
+        args.append(source)
+    args += [prev, now, core, cross] + list(quant)
     if mode == "bwd":
         args.append(planes)
     args += list(fields) + list(tables)
@@ -276,9 +292,9 @@
     return call(functools.partial(step_kernel, mode, first, moment), args, outs, scratch, "step_" + mode)
 
 
-def blocks_kernel(ids, begin, part, a5, s0, a0, s5, b0, b1, b2, b3):
+def blocks_kernel(ids, part, a5, s0, a0, s5, b0, b1, b2, b3):
     ring, _ = ring_of(ids)
-    first, offset = begin[0] >> 6, begin[0] & 63
+    first, offset = ids[2] >> 6, ids[2] & 63
     within = lax.broadcasted_iota(jnp.int32, (TILE, COLS), 0)
     column = lax.broadcasted_iota(jnp.int32, (TILE, COLS), 1) + offset
     picks = [jnp.where(within + ((ring + s - first) & 3) * TILE == column, 1.0, 0.0) for s in range(4)]
@@ -293,8 +309,8 @@
             block[r] = placed[s * TILE : (s + 1) * TILE]
 
 
-def combine_kernel(ids, begin, s1, s2, s3, b0, b1, b2, b3, keep, give):
-    flags = [jnp.where(serves_upper(start[0], ids), 1.0, 0.0).astype(F32) for start in (begin, s1, s2, s3)]
+def combine_kernel(ids, b0, b1, b2, b3, keep, give):
+    flags = [jnp.where(serves_upper(ids[i], ids), 1.0, 0.0).astype(F32) for i in (2, 4, 5, 6)]
     for r in range(ROWS):
         kept = flags[0] * b0[r]
         total = b0[r]
@@ -326,7 +342,6 @@
     count = lax.axis_size("apert")
     groups = lax.axis_size("shot")
     half = groups // 2
-    parity = place & 1
     ids = jnp.stack([place, shot]).astype(jnp.int32)
     core_pairs = [(i, i ^ 1) for i in range(count)]
     cross_pairs = [(i, i + 1) for i in range(1, count - 1, 2)] + [(i + 1, i) for i in range(1, count - 1, 2)]
@@ -335,36 +350,45 @@
     def ring_pairs(shift):
         return [(i, (i // half) * half + (i % half + shift) % half) for i in range(groups)]
 
-    def faces(field):
-        return (
-            lax.dynamic_slice_in_dim(field, (1 - parity) * 4, 4, 0),
-            lax.dynamic_slice_in_dim(field, parity * 4, 4, 0),
-        )
-
     def swap(core, cross):
         return lax.ppermute(core, "apert", core_pairs), lax.ppermute(cross, "apert", cross_pairs)
+
+    both_ways = [
+        (i * count + j, ((i // half) * half + (i % half + (1 if j % 2 == 0 else -1)) % half) * count + j)
+        for i in range(groups)
+        for j in range(count)
+    ]
+
+    def ring_send(pieces):
+        halfway = lax.ppermute(pieces[2], ("shot", "apert"), both_ways)
+        near = lax.ppermute(pieces[1], "shot", ring_pairs(1)), lax.ppermute(pieces[3], "shot", ring_pairs(3))
+        return [pieces[0], near[0], lax.ppermute(halfway, ("shot", "apert"), both_ways), near[1]]
 
     starts = [lax.ppermute(anchors, "shot", ring_pairs(k)) for k in range(1, half)]
     other_vel = lax.ppermute(velocity, "shot", side_pairs)
     other_dens = lax.ppermute(density, "shot", side_pairs)
+    fwd_prev, fwd_now, bwd_prev, bwd_now = forward_prev[0], forward_now[0], adjoint_prev[0], adjoint_now[0]
+    pair = ((2,) + FACE, F32)
+    tile = ((ROWS, TILE, DEPTH), BF16)
+    core_faces, cross_faces, own_fwd, own_bwd, vel, dens = call(
+        faces_kernel,
+        [ids, fwd_now, bwd_now, velocity, density],
+        [pair, ((2, 5, COLS, DEPTH), BF16), (FACE, F32), (FACE, F32), tile, tile],
+        name="faces",
+    )
+    nums = jnp.concatenate([ids, anchors, shot_cell, *starts])
     tile2 = ((2, ROWS, TILE, DEPTH), BF16)
-    tiles = call(
-        select_kernel, [ids, anchors, *starts, velocity, density, other_vel, other_dens], [tile2] * half, name="select"
-    )
-    tiles = [tiles[0]] + [lax.ppermute(tiles[k], "shot", ring_pairs(k)) for k in range(1, half)]
-
-    fwd_prev, fwd_now, bwd_prev, bwd_now = forward_prev[0], forward_now[0], adjoint_prev[0], adjoint_now[0]
-    fwd_faces, bwd_faces = faces(fwd_now), faces(bwd_now)
-    fwd_core, fwd_cross = swap(*fwd_faces)
-    bwd_core, bwd_cross = swap(*bwd_faces)
+    tiles = call(select_kernel, [nums, vel, dens, other_vel, other_dens], [tile2] * half, name="select")
+    tiles = ring_send(tiles)
+    first_core, first_cross = swap(core_faces, cross_faces)
 
     wide = [pltpu.VMEM((ROWS, 4 * TILE, DEPTH), BF16)]
     dens, dens_core, dens_cross = call(
-        window_dens_kernel, [ids, anchors, *tiles], [(SLAB, F32), (FACE, BF16), (FACE, BF16)], wide, "window_dens"
+        window_dens_kernel, [nums, *tiles], [(SLAB, F32), (FACE, BF16), (FACE, BF16)], wide, "window_dens"
     )
     dens_core, dens_cross = swap(dens_core, dens_cross)
     coef, slope1, slope2, logs = call(
-        coef_kernel, [ids, anchors, *tiles, dens, *tables], [(SLAB, F32)] * 4, wide, "coef"
+        coef_kernel, [nums, *tiles, dens, *tables], [(SLAB, F32)] * 4, wide, "coef"
     )
     (slope0,) = call(
         row_slope_kernel,
@@ -376,19 +400,21 @@
     fields = (coef, slope0, slope1, slope2)
     lane = lax.broadcasted_iota(jnp.int32, (1, 1, 1, 128), 3)
     planes = jnp.where(lane == SURF, records[0][..., None], 0.0)
-    source = (shot_cell, wavelet[0])
-
-    fwd_quant = bwd_quant = None
+    source = wavelet[0]
+
+    fwd_core = bwd_core = first_core
+    fwd_cross = bwd_cross = first_cross
+    fwd_quant, bwd_quant = (own_fwd,), (own_bwd,)
     snapshots, states = [], []
     for moment in range(STEPS):
         last = moment == STEPS - 1
         if moment > 0:
             fwd_core, fwd_cross = swap(fwd_core, fwd_cross)
         new, *sent = step(
-            "fwd", moment, ids, source, fwd_prev, fwd_now, fwd_core, fwd_cross, fwd_quant, None, fields, tables
+            "fwd", moment, nums, source, fwd_prev, fwd_now, fwd_core, fwd_cross, fwd_quant, None, fields, tables
         )
         if not last:
-            own = fwd_faces[1] if moment == 0 else fwd_quant[2]
+            own = own_fwd if moment == 0 else fwd_quant[2]
             fwd_core, fwd_cross, seen, shown = sent
             fwd_quant = (seen, seen if moment == 0 else fwd_quant[0], shown, own)
         snapshots.append(new)
@@ -397,10 +423,10 @@
         if moment > 0:
             bwd_core, bwd_cross = swap(bwd_core, bwd_cross)
         new, *sent = step(
-            "bwd", moment, ids, source, bwd_prev, bwd_now, bwd_core, bwd_cross, bwd_quant, planes, fields, tables
+            "bwd", moment, nums, source, bwd_prev, bwd_now, bwd_core, bwd_cross, bwd_quant, planes, fields, tables
         )
         if not last:
-            own = bwd_faces[1] if moment == 0 else bwd_quant[2]
+            own = own_bwd if moment == 0 else bwd_quant[2]
             bwd_core, bwd_cross, seen, shown = sent
             bwd_quant = (seen, seen if moment == 0 else bwd_quant[0], shown, own)
         states.append(new)
@@ -410,12 +436,12 @@
     block = ((ROWS, TILE, DEPTH), F32)
     blocks = call(
         blocks_kernel,
-        [ids, anchors, part, states[STEPS - 1], snapshots[0], states[0], snapshots[STEPS - 1]],
+        [nums, part, states[STEPS - 1], snapshots[0], states[0], snapshots[STEPS - 1]],
         [block] * half,
         name="blocks",
     )
-    arrived = [blocks[0]] + [lax.ppermute(blocks[k], "shot", ring_pairs(k)) for k in range(1, half)]
-    keep, give = call(combine_kernel, [ids, anchors, *starts, *arrived], [block] * 2, name="combine")
+    arrived = ring_send(blocks)
+    keep, give = call(combine_kernel, [nums, *arrived], [block] * 2, name="combine")
     image = keep + lax.ppermute(give, "shot", side_pairs)
     return image, states[STEPS - 1][None]
 

time: 270 us -> 228 us (0.84)
  waiting for transfers between devices: 102 us -> 56.5 us
  local copies, waits for them, and re-layouts: 4.54 us -> 12.6 us
  Pallas kernels: 79.5 us -> 75.9 us
    ppermute x13 -> x12, waiting for transfers between devices: 51.9 us -> 14.8 us  [swap(): lax.ppermute(cross, 'apert', cross_pairs)]
    unnamed x21 -> x41, local copies, waits for them, and re-layouts: 3.09 us -> 10.7 us
    ppermute x1, waiting for transfers between devices: 4.9 us -> 0.01 us  [shards(): other_dens = lax.ppermute(density, 'shot', side_pairs)]
    ppermute x13 -> x12, starting transfers between devices: 52.2 us -> 56.2 us  [swap(): lax.ppermute(cross, 'apert', cross_pairs)]
    ppermute x13 -> x12, starting transfers between devices: 6.52 us -> 2.89 us  [swap(): lax.ppermute(core, 'apert', core_pairs)]
    pallas_call x18 -> x19, Pallas kernels: 79.5 us -> 75.9 us  [call(): pl.pallas_call(body, out_shape=[pltpu.VMEM(shape, dtype) for shape, dtype...]
    ppermute x6 -> x8, waiting for transfers between devices: 32.7 us -> 29.1 us  [the longest x2 16.6 us: ring_send(): halfway = lax.ppermute(pieces[2], ('shot', 'apert'), both_ways)]
    ppermute x6 -> x8, starting transfers between devices: 9.21 us -> 10 us  [the longest x2 3.97 us: ring_send(): lax.ppermute(pieces[3], 'shot', ring_pairs(3))]
  transfers between devices with their start and end apart: 38 -> 38, of which waited for: 20 -> 9; matrix products, arithmetic and copies ran while one was open for 2% -> 2% of each run, Pallas kernels for 25% -> 27%
where the time goes in v3:
time: 228 us; the launch traced here: 227 us
  starting transfers between devices  76.6 us (34%)
  Pallas kernels  75.9 us (33%)
  waiting for transfers between devices  56.5 us (25%)
  local copies, waits for them, and re-layouts  12.6 us (6%)
  other arithmetic  2.73 us (1%)
  between operations  2.57 us (1%)
    pallas_call x19, Pallas kernels, call(): pl.pallas_call(body, out_shape=[pltpu.VMEM(shape, dtype) for shape, dtype...  75.9 us
    ppermute x12, starting transfers between devices, swap(): lax.ppermute(cross, 'apert', cross_pairs)  56.2 us
    ppermute x2, waiting for transfers between devices, ring_send(): halfway = lax.ppermute(pieces[2], ('shot', 'apert'), both_ways)  16.6 us
    ppermute x12, waiting for transfers between devices, swap(): lax.ppermute(cross, 'apert', cross_pairs)  14.8 us
    ppermute x1, waiting for transfers between devices, shards(): image = keep + lax.ppermute(give, 'shot', side_pairs)  12.5 us
    unnamed x41, local copies, waits for them, and re-layouts  10.7 us
    ppermute x2, waiting for transfers between devices, ring_send(): lax.ppermute(halfway, ('shot', 'apert'), both_ways)  8.93 us
    ppermute x3, starting transfers between devices, shards(): lax.ppermute(anchors, 'shot', ring_pairs(k))  5.67 us
  transfers between devices with their start and end apart: 38, of which 9 were waited for; matrix products, arithmetic and copies ran while one was open for 2% of the time, Pallas kernels for 27%

profile of v3, /device:TPU:7, one launch (start us, length us, event | category | flops | bytes accessed | tf_op | source)
XLA Modules:
  0.0 226.9 jit_solution(15039983611064362296)
XLA Ops:
  24.3 8.4 %collective-permute-done.8 = bf16[2,8,64,256]{3,2,1,0:T(8,128)(2,1)S(1)} collective-permute-done((bf16[2,8,64,256]{3,2,1,0:T(8,128)(2,1)S(1)}, bf16[2,8,64,256]{3,2,1,0:T(8,128)(2,1)S(1)}, u32[]{:S(2)}, u32[]{:S(2)}) %collective-permute-start.8) | collective-permute-done | bytes 524320 | tf_op jit(solution)/shard_map/ppermute | solution.py:363
  32.7 9.2 %collective-permute-start.4 = (bf16[2,5,160,256]{3,2,1,0:T(8,128)(2,1)S(1)}, bf16[2,5,160,256]{3,2,1,0:T(8,128)(2,1)S(1)}, u32[]{:S(2)}, u32[]{:S(2)}) collective-permute-start(bf16[2,5,160,256]{3,2,1,0:T(8,128)(2,1)S(1)} %get-tuple-element.76), channel_id=1, source_target_pairs={{1,2},{3,4},{5,6},{7,8},{9,10},{11,12},{13,14},{2,1},{4,3},{6,5},{... | collective-permute-start | bytes 2457608 | tf_op jit(solution)/shard_map/ppermute | solution.py:354
  49.5 4.3 %collective-permute-start.12 = (bf16[4,160,256]{2,1,0:T(8,128)(2,1)S(1)}, bf16[4,160,256]{2,1,0:T(8,128)(2,1)S(1)}, u32[]{:S(2)}, u32[]{:S(2)}) collective-permute-start(bf16[4,160,256]{2,1,0:T(8,128)(2,1)S(1)} %get-tuple-element.88), channel_id=1, source_target_pairs={{1,2},{3,4},{5,6},{7,8},{9,10},{11,12},{13,14},{2,1},{4,3},{6,5},{... | collective-permute-start | bytes 983048 | tf_op jit(solution)/shard_map/ppermute | solution.py:354
  55.5 10.5 %collective-permute-done.12.cross = bf16[4,160,256]{2,1,0:T(8,128)(2,1)S(1)} collective-permute-done((bf16[4,160,256]{2,1,0:T(8,128)(2,1)S(1)}, bf16[4,160,256]{2,1,0:T(8,128)(2,1)S(1)}, u32[]{:S(2)}, u32[]{:S(2)}) %collective-permute-start.12) | collective-permute-done | bytes 327712 | tf_op jit(solution)/shard_map/ppermute | solution.py:354
  67.8 5.6 %step_bwd.6 = (f32[8,160,256]{2,1,0:T(8,128)S(1)}, f32[4,160,256]{2,1,0:T(8,128)S(1)}, bf16[4,160,256]{2,1,0:T(8,128)(2,1)S(1)}, f32[4,160,256]{2,1,0:T(8,128)S(1)}, f32[4,160,256]{2,1,0:T(8,128)S(1)}) custom-call(s32[7]{0:T(128)S(1)} %concatenate.4.ids.refs_0_, f32[8,160,256]{2,1,0:T(8,128)S(1)} %bitcast.10, f32[8,160,256]{2,1,0:T(8,128)S(1)} %bitcast.13, ...), custom_call_target="tpu_custom_call" | custom-call | flops 20000000000 | bytes 100000 | tf_op jit(solution)/shard_map/step_bwd/pallas_call | solution.py:77
  73.4 5.5 %collective-permute-start.14 = (bf16[4,160,256]{2,1,0:T(8,128)(2,1)S(1)}, bf16[4,160,256]{2,1,0:T(8,128)(2,1)S(1)}, u32[]{:S(2)}, u32[]{:S(2)}) collective-permute-start(bf16[4,160,256]{2,1,0:T(8,128)(2,1)S(1)} %get-tuple-element.93), channel_id=1, source_target_pairs={{1,2},{3,4},{5,6},{7,8},{9,10},{11,12},{13,14},{2,1},{4,3},{6,5},{... | collective-permute-start | bytes 983048 | tf_op jit(solution)/shard_map/ppermute | solution.py:354
  79.0 5.5 %step_fwd.6 = (f32[8,160,256]{2,1,0:T(8,128)S(1)}, f32[4,160,256]{2,1,0:T(8,128)S(1)}, bf16[4,160,256]{2,1,0:T(8,128)(2,1)S(1)}, f32[4,160,256]{2,1,0:T(8,128)S(1)}, f32[4,160,256]{2,1,0:T(8,128)S(1)}) custom-call(s32[7]{0:T(128)S(1)} %concatenate.4.ids.refs_0_, f32[6]{0:T(128)S(1)} %bitcast.18, f32[8,160,256]{2,1,0:T(8,128)S(1)} %bitcast.11, ...), custom_call_target="tpu_custom_call" | custom-call | flops 20000000000 | bytes 100000 | tf_op jit(solution)/shard_map/step_fwd/pallas_call | solution.py:77
  88.5 5.8 %step_bwd.7 = (f32[8,160,256]{2,1,0:T(8,128)S(1)}, f32[4,160,256]{2,1,0:T(8,128)S(1)}, bf16[4,160,256]{2,1,0:T(8,128)(2,1)S(1)}, f32[4,160,256]{2,1,0:T(8,128)S(1)}, f32[4,160,256]{2,1,0:T(8,128)S(1)}) custom-call(s32[7]{0:T(128)S(1)} %concatenate.4.ids.refs_0_, f32[8,160,256]{2,1,0:T(8,128)S(1)} %bitcast.14, ...), custom_call_target="tpu_custom_call" | custom-call | flops 20000000000 | bytes 100000 | tf_op jit(solution)/shard_map/step_bwd/pallas_call | solution.py:77
  94.3 5.0 %collective-permute-start.24 = (bf16[4,160,256]{2,1,0:T(8,128)(2,1)S(1)}, bf16[4,160,256]{2,1,0:T(8,128)(2,1)S(1)}, u32[]{:S(2)}, u32[]{:S(2)}) collective-permute-start(bf16[4,160,256]{2,1,0:T(8,128)(2,1)S(1)} %get-tuple-element.120), channel_id=1, source_target_pairs={{1,2},{3,4},{5,6},{7,8},{9,10},{11,12},{13,14},{2,1},{4,3},{6,5},{... | collective-permute-start | bytes 983048 | tf_op jit(solution)/shard_map/ppermute | solution.py:354
  99.6 5.7 %step_fwd.7 = (f32[8,160,256]{2,1,0:T(8,128)S(1)}, f32[4,160,256]{2,1,0:T(8,128)S(1)}, bf16[4,160,256]{2,1,0:T(8,128)(2,1)S(1)}, f32[4,160,256]{2,1,0:T(8,128)S(1)}, f32[4,160,256]{2,1,0:T(8,128)S(1)}) custom-call(s32[7]{0:T(128)S(1)} %concatenate.4.ids.refs_0_, f32[6]{0:T(128)S(1)} %bitcast.19, f32[8,160,256]{2,1,0:T(8,128)S(1)} %bitcast.17, ...), custom_call_target="tpu_custom_call" | custom-call | flops 20000000000 | bytes 100000 | tf_op jit(solution)/shard_map/step_fwd/pallas_call | solution.py:77
  109.3 5.7 %step_bwd.8 = (f32[8,160,256]{2,1,0:T(8,128)S(1)}, f32[4,160,256]{2,1,0:T(8,128)S(1)}, bf16[4,160,256]{2,1,0:T(8,128)(2,1)S(1)}, f32[4,160,256]{2,1,0:T(8,128)S(1)}, f32[4,160,256]{2,1,0:T(8,128)S(1)}) custom-call(s32[7]{0:T(128)S(1)} %concatenate.4.ids.refs_0_, f32[8,160,256]{2,1,0:T(8,128)S(1)} %get-tuple-element.91.refs_2_.refs_1_.a0, ...), custom_call_target="tpu_custom_call" | custom-call | flops 20000000000 | bytes 100000 | tf_op jit(solution)/shard_map/step_bwd/pallas_call | solution.py:77
  115.0 5.0 %collective-permute-start.26 = (bf16[4,160,256]{2,1,0:T(8,128)(2,1)S(1)}, bf16[4,160,256]{2,1,0:T(8,128)(2,1)S(1)}, u32[]{:S(2)}, u32[]{:S(2)}) collective-permute-start(bf16[4,160,256]{2,1,0:T(8,128)(2,1)S(1)} %get-tuple-element.125), channel_id=1, source_target_pairs={{1,2},{3,4},{5,6},{7,8},{9,10},{11,12},{13,14},{2,1},{4,3},{6,5},{... | collective-permute-start | bytes 983048 | tf_op jit(solution)/shard_map/ppermute | solution.py:354
  120.1 5.7 %step_fwd.8 = (f32[8,160,256]{2,1,0:T(8,128)S(1)}, f32[4,160,256]{2,1,0:T(8,128)S(1)}, bf16[4,160,256]{2,1,0:T(8,128)(2,1)S(1)}, f32[4,160,256]{2,1,0:T(8,128)S(1)}, f32[4,160,256]{2,1,0:T(8,128)S(1)}) custom-call(s32[7]{0:T(128)S(1)} %concatenate.4.ids.refs_0_, f32[6]{0:T(128)S(1)} %bitcast.20, f32[8,160,256]{2,1,0:T(8,128)S(1)} %get-tuple-element.98.refs_3_.refs_2_.s0, ...), custom_call_target="tpu_custom_call" | custom-call | flops 20000000000 | bytes 100000 | tf_op jit(solution)/shard_map/step_fwd/pallas_call | solution.py:77
  129.5 5.7 %step_bwd.9 = (f32[8,160,256]{2,1,0:T(8,128)S(1)}, f32[4,160,256]{2,1,0:T(8,128)S(1)}, bf16[4,160,256]{2,1,0:T(8,128)(2,1)S(1)}, f32[4,160,256]{2,1,0:T(8,128)S(1)}, f32[4,160,256]{2,1,0:T(8,128)S(1)}) custom-call(s32[7]{0:T(128)S(1)} %concatenate.4.ids.refs_0_, f32[8,160,256]{2,1,0:T(8,128)S(1)} %get-tuple-element.96.refs_2_.refs_1_, ...), custom_call_target="tpu_custom_call" | custom-call | flops 20000000000 | bytes 100000 | tf_op jit(solution)/shard_map/step_bwd/pallas_call | solution.py:77
  135.2 4.4 %collective-permute-start.28 = (bf16[4,160,256]{2,1,0:T(8,128)(2,1)S(1)}, bf16[4,160,256]{2,1,0:T(8,128)(2,1)S(1)}, u32[]{:S(2)}, u32[]{:S(2)}) collective-permute-start(bf16[4,160,256]{2,1,0:T(8,128)(2,1)S(1)} %get-tuple-element.130), channel_id=1, source_target_pairs={{1,2},{3,4},{5,6},{7,8},{9,10},{11,12},{13,14},{2,1},{4,3},{6,5},{... | collective-permute-start | bytes 983048 | tf_op jit(solution)/shard_map/ppermute | solution.py:354
  139.8 5.8 %step_fwd.9 = (f32[8,160,256]{2,1,0:T(8,128)S(1)}, f32[4,160,256]{2,1,0:T(8,128)S(1)}, bf16[4,160,256]{2,1,0:T(8,128)(2,1)S(1)}, f32[4,160,256]{2,1,0:T(8,128)S(1)}, f32[4,160,256]{2,1,0:T(8,128)S(1)}) custom-call(s32[7]{0:T(128)S(1)} %concatenate.4.ids.refs_0_, f32[6]{0:T(128)S(1)} %bitcast.21, f32[8,160,256]{2,1,0:T(8,128)S(1)} %get-tuple-element.103.refs_3_.refs_2_, ...), custom_call_target="tpu_custom_call" | custom-call | flops 20000000000 | bytes 100000 | tf_op jit(solution)/shard_map/step_fwd/pallas_call | solution.py:77
  149.2 5.8 %step_bwd.10 = (f32[8,160,256]{2,1,0:T(8,128)S(1)}, f32[4,160,256]{2,1,0:T(8,128)S(1)}, bf16[4,160,256]{2,1,0:T(8,128)(2,1)S(1)}, f32[4,160,256]{2,1,0:T(8,128)S(1)}, f32[4,160,256]{2,1,0:T(8,128)S(1)}) custom-call(s32[7]{0:T(128)S(1)} %concatenate.4.ids.refs_0_, f32[8,160,256]{2,1,0:T(8,128)S(1)} %get-tuple-element.123.refs_2_.refs_1_, ...), custom_call_target="tpu_custom_call" | custom-call | flops 20000000000 | bytes 100000 | tf_op jit(solution)/shard_map/step_bwd/pallas_call | solution.py:77
  155.0 4.6 %collective-permute-start.30 = (bf16[4,160,256]{2,1,0:T(8,128)(2,1)S(1)}, bf16[4,160,256]{2,1,0:T(8,128)(2,1)S(1)}, u32[]{:S(2)}, u32[]{:S(2)}) collective-permute-start(bf16[4,160,256]{2,1,0:T(8,128)(2,1)S(1)} %get-tuple-element.135), channel_id=1, source_target_pairs={{1,2},{3,4},{5,6},{7,8},{9,10},{11,12},{13,14},{2,1},{4,3},{6,5},{... | collective-permute-start | bytes 983048 | tf_op jit(solution)/shard_map/ppermute | solution.py:354
  159.7 5.7 %step_fwd.10 = (f32[8,160,256]{2,1,0:T(8,128)S(1)}, f32[4,160,256]{2,1,0:T(8,128)S(1)}, bf16[4,160,256]{2,1,0:T(8,128)(2,1)S(1)}, f32[4,160,256]{2,1,0:T(8,128)S(1)}, f32[4,160,256]{2,1,0:T(8,128)S(1)}) custom-call(s32[7]{0:T(128)S(1)} %concatenate.4.ids.refs_0_, f32[6]{0:T(128)S(1)} %bitcast.22, f32[8,160,256]{2,1,0:T(8,128)S(1)} %get-tuple-element.108.refs_3_.refs_2_, ...), custom_call_target="tpu_custom_call" | custom-call | flops 20000000000 | bytes 100000 | tf_op jit(solution)/shard_map/step_fwd/pallas_call | solution.py:77
  170.6 5.4 %step_bwd.11.a5 = f32[8,160,256]{2,1,0:T(8,128)S(1)} custom-call(s32[7]{0:T(128)S(1)} %concatenate.4.ids.refs_0_, f32[8,160,256]{2,1,0:T(8,128)S(1)} %get-tuple-element.128.refs_2_.refs_1_, f32[8,160,256]{2,1,0:T(8,128)S(1)} %get-tuple-element.133.refs_2_, f32[4,160,256]{2,1,0:T(8,128)S(1)} %collective-permute-done.29.refs_3_, ...), custom_call_target="tpu_custom_call" | custom-call | flops 20000000000 | bytes 100000 | tf_op jit(solution)/shard_map/step_bwd/pallas_call | solution.py:77
  180.2 5.3 %step_fwd.11.s5 = f32[8,160,256]{2,1,0:T(8,128)S(1)} custom-call(s32[7]{0:T(128)S(1)} %concatenate.4.ids.refs_0_, f32[6]{0:T(128)S(1)} %bitcast.23, f32[8,160,256]{2,1,0:T(8,128)S(1)} %get-tuple-element.113.refs_3_.refs_2_, f32[8,160,256]{2,1,0:T(8,128)S(1)} %get-tuple-element.118.refs_3_, f32[4,160,256]{2,1,0:T(8,128)S(1)} %collective-permute-done.31.refs_4_, ...), custom_call_target="tpu_custom_call" | custom-call | flops 20000000000 | bytes 100000 | tf_op jit(solution)/shard_map/step_fwd/pallas_call | solution.py:77
  192.2 8.2 %collective-permute-done.34 = f32[8,64,256]{2,1,0:T(8,128)S(1)} collective-permute-done((f32[8,64,256]{2,1,0:T(8,128)S(1)}, f32[8,64,256]{2,1,0:T(8,128)S(1)}, u32[]{:S(2)}, u32[]{:S(2)}) %collective-permute-start.34) | collective-permute-done | bytes 524320 | tf_op jit(solution)/shard_map/ppermute | solution.py:363
  206.0 5.3 %collective-permute-done.35.b2 = f32[8,64,256]{2,1,0:T(8,128)S(1)} collective-permute-done((f32[8,64,256]{2,1,0:T(8,128)S(1)}, f32[8,64,256]{2,1,0:T(8,128)S(1)}, u32[]{:S(2)}, u32[]{:S(2)}) %collective-permute-start.35) | collective-permute-done | bytes 524320 | tf_op jit(solution)/shard_map/ppermute | solution.py:365
  213.5 12.5 %collective-permute-done.37 = f32[8,64,256]{2,1,0:T(8,128)S(1)} collective-permute-done((f32[8,64,256]{2,1,0:T(8,128)S(1)}, f32[8,64,256]{2,1,0:T(8,128)S(1)}, u32[]{:S(2)}, u32[]{:S(2)}) %collective-permute-start.37) | collective-permute-done | bytes 524320 | tf_op jit(solution)/shard_map/ppermute | solution.py:445
  (118 shorter events, 73.7 us)
Async XLA Ops:
  0.6 16.2 %collective-permute-start.1 = (s32[1]{0:T(128)}, s32[1]{0:T(128)}, u32[]{:S(2)}, u32[]{:S(2)}) collective-permute-start(s32[1]{0:T(128)} %param.18), channel_id=1, source_target_pairs={{0,32},{16,48},{32,0},{48,16},{64,96},{80,112},{96,64},{112,80},{1... | collective-permute-start | bytes 20 | tf_op jit(solution)/shard_map/ppermute | solution.py:367
  3.6 13.3 %collective-permute-start = (s32[1]{0:T(128)}, s32[1]{0:T(128)}, u32[]{:S(2)}, u32[]{:S(2)}) collective-permute-start(s32[1]{0:T(128)} %param.18), channel_id=1, source_target_pairs={{0,16},{16,32},{32,48},{48,0},{64,80},{80,96},{96,112},{112,64},{1... | collective-permute-start | bytes 20 | tf_op jit(solution)/shard_map/ppermute | solution.py:367
  4.0 12.9 %collective-permute-start.2 = (s32[1]{0:T(128)}, s32[1]{0:T(128)}, u32[]{:S(2)}, u32[]{:S(2)}) collective-permute-start(s32[1]{0:T(128)} %param.18), channel_id=1, source_target_pairs={{0,48},{16,0},{32,16},{48,32},{64,112},{80,64},{96,80},{112,96},{1... | collective-permute-start | bytes 20 | tf_op jit(solution)/shard_map/ppermute | solution.py:367
  6.3 12.5 %collective-permute-start.5 = (bf16[8,64,256]{2,1,0:T(8,128)(2,1)}, bf16[8,64,256]{2,1,0:T(8,128)(2,1)S(1)}, u32[]{:S(2)}, u32[]{:S(2)}) collective-permute-start(bf16[8,64,256]{2,1,0:T(8,128)(2,1)} %vel.1), channel_id=1, source_target_pairs={{0,64},{16,80},{32,96},{48,112},{64,0},{80,16},{96,32},{112,48},{1... | collective-permute-start | bytes 786440 | tf_op jit(solution)/shard_map/ppermute | solution.py:368
  21.5 21.5 %collective-permute-start.7 = (bf16[2,8,64,256]{3,2,1,0:T(8,128)(2,1)S(1)}, bf16[2,8,64,256]{3,2,1,0:T(8,128)(2,1)S(1)}, u32[]{:S(2)}, u32[]{:S(2)}) collective-permute-start(bf16[2,8,64,256]{3,2,1,0:T(8,128)(2,1)S(1)} %get-tuple-element.81), channel_id=1, source_target_pairs={{0,16},{16,32},{32,48},{48,0},{64,80},{80,96},{96,112},{112,64},{1... | collective-permute-start | bytes 1572872 | tf_op jit(solution)/shard_map/ppermute | solution.py:364
  23.0 20.1 %collective-permute-start.10 = (bf16[2,8,64,256]{3,2,1,0:T(8,128)(2,1)S(1)}, bf16[2,8,64,256]{3,2,1,0:T(8,128)(2,1)S(1)}, u32[]{:S(2)}, u32[]{:S(2)}) collective-permute-start(bf16[2,8,64,256]{3,2,1,0:T(8,128)(2,1)S(1)} %get-tuple-element.83), channel_id=1, source_target_pairs={{0,48},{16,0},{32,16},{48,32},{64,112},{80,64},{96,80},{112,96},{1... | collective-permute-start | bytes 1572872 | tf_op jit(solution)/shard_map/ppermute | solution.py:364
  32.7 14.0 %collective-permute-start.9 = (bf16[2,8,64,256]{3,2,1,0:T(8,128)(2,1)S(1)}, bf16[2,8,64,256]{3,2,1,0:T(8,128)(2,1)S(1)}, u32[]{:S(2)}, u32[]{:S(2)}) collective-permute-start(bf16[2,8,64,256]{3,2,1,0:T(8,128)(2,1)S(1)} %collective-permute-done.8), channel_id=1, source_target_pairs={{0,16},{1,49},{2,18},{3,51},{4,20},{5,53},{6,22},{7,55},{8,24},{9,... | collective-permute-start | bytes 1572872 | tf_op jit(solution)/shard_map/ppermute | solution.py:365
  32.7 35.0 %collective-permute-start.4 = (bf16[2,5,160,256]{3,2,1,0:T(8,128)(2,1)S(1)}, bf16[2,5,160,256]{3,2,1,0:T(8,128)(2,1)S(1)}, u32[]{:S(2)}, u32[]{:S(2)}) collective-permute-start(bf16[2,5,160,256]{3,2,1,0:T(8,128)(2,1)S(1)} %get-tuple-element.76), channel_id=1, source_target_pairs={{1,2},{3,4},{5,6},{7,8},{9,10},{11,12},{13,14},{2,1},{4,3},{6,5},{... | collective-permute-start | bytes 2457608 | tf_op jit(solution)/shard_map/ppermute | solution.py:354
  41.9 25.8 %collective-permute-start.3 = (f32[2,4,160,256]{3,2,1,0:T(8,128)S(1)}, f32[2,4,160,256]{3,2,1,0:T(8,128)S(1)}, u32[]{:S(2)}, u32[]{:S(2)}) collective-permute-start(f32[2,4,160,256]{3,2,1,0:T(8,128)S(1)} %get-tuple-element.75), channel_id=1, source_target_pairs={{0,1},{1,0},{2,3},{3,2},{4,5},{5,4},{6,7},{7,6},{8,9},{9,8},{10,11... | collective-permute-start | bytes 3932168 | tf_op jit(solution)/shard_map/ppermute | solution.py:354
  49.5 16.5 %collective-permute-start.12 = (bf16[4,160,256]{2,1,0:T(8,128)(2,1)S(1)}, bf16[4,160,256]{2,1,0:T(8,128)(2,1)S(1)}, u32[]{:S(2)}, u32[]{:S(2)}) collective-permute-start(bf16[4,160,256]{2,1,0:T(8,128)(2,1)S(1)} %get-tuple-element.88), channel_id=1, source_target_pairs={{1,2},{3,4},{5,6},{7,8},{9,10},{11,12},{13,14},{2,1},{4,3},{6,5},{... | collective-permute-start | bytes 983048 | tf_op jit(solution)/shard_map/ppermute | solution.py:354
  73.4 15.1 %collective-permute-start.14 = (bf16[4,160,256]{2,1,0:T(8,128)(2,1)S(1)}, bf16[4,160,256]{2,1,0:T(8,128)(2,1)S(1)}, u32[]{:S(2)}, u32[]{:S(2)}) collective-permute-start(bf16[4,160,256]{2,1,0:T(8,128)(2,1)S(1)} %get-tuple-element.93), channel_id=1, source_target_pairs={{1,2},{3,4},{5,6},{7,8},{9,10},{11,12},{13,14},{2,1},{4,3},{6,5},{... | collective-permute-start | bytes 983048 | tf_op jit(solution)/shard_map/ppermute | solution.py:354
  84.5 15.0 %collective-permute-start.16 = (bf16[4,160,256]{2,1,0:T(8,128)(2,1)S(1)}, bf16[4,160,256]{2,1,0:T(8,128)(2,1)S(1)}, u32[]{:S(2)}, u32[]{:S(2)}) collective-permute-start(bf16[4,160,256]{2,1,0:T(8,128)(2,1)S(1)} %get-tuple-element.100), channel_id=1, source_target_pairs={{1,2},{3,4},{5,6},{7,8},{9,10},{11,12},{13,14},{2,1},{4,3},{6,5},{... | collective-permute-start | bytes 983048 | tf_op jit(solution)/shard_map/ppermute | solution.py:354
  94.3 15.0 %collective-permute-start.24 = (bf16[4,160,256]{2,1,0:T(8,128)(2,1)S(1)}, bf16[4,160,256]{2,1,0:T(8,128)(2,1)S(1)}, u32[]{:S(2)}, u32[]{:S(2)}) collective-permute-start(bf16[4,160,256]{2,1,0:T(8,128)(2,1)S(1)} %get-tuple-element.120), channel_id=1, source_target_pairs={{1,2},{3,4},{5,6},{7,8},{9,10},{11,12},{13,14},{2,1},{4,3},{6,5},{... | collective-permute-start | bytes 983048 | tf_op jit(solution)/shard_map/ppermute | solution.py:354
  105.3 14.8 %collective-permute-start.18 = (bf16[4,160,256]{2,1,0:T(8,128)(2,1)S(1)}, bf16[4,160,256]{2,1,0:T(8,128)(2,1)S(1)}, u32[]{:S(2)}, u32[]{:S(2)}) collective-permute-start(bf16[4,160,256]{2,1,0:T(8,128)(2,1)S(1)} %get-tuple-element.105), channel_id=1, source_target_pairs={{1,2},{3,4},{5,6},{7,8},{9,10},{11,12},{13,14},{2,1},{4,3},{6,5},{... | collective-permute-start | bytes 983048 | tf_op jit(solution)/shard_map/ppermute | solution.py:354
  115.0 14.5 %collective-permute-start.26 = (bf16[4,160,256]{2,1,0:T(8,128)(2,1)S(1)}, bf16[4,160,256]{2,1,0:T(8,128)(2,1)S(1)}, u32[]{:S(2)}, u32[]{:S(2)}) collective-permute-start(bf16[4,160,256]{2,1,0:T(8,128)(2,1)S(1)} %get-tuple-element.125), channel_id=1, source_target_pairs={{1,2},{3,4},{5,6},{7,8},{9,10},{11,12},{13,14},{2,1},{4,3},{6,5},{... | collective-permute-start | bytes 983048 | tf_op jit(solution)/shard_map/ppermute | solution.py:354
  125.8 13.9 %collective-permute-start.20 = (bf16[4,160,256]{2,1,0:T(8,128)(2,1)S(1)}, bf16[4,160,256]{2,1,0:T(8,128)(2,1)S(1)}, u32[]{:S(2)}, u32[]{:S(2)}) collective-permute-start(bf16[4,160,256]{2,1,0:T(8,128)(2,1)S(1)} %get-tuple-element.110), channel_id=1, source_target_pairs={{1,2},{3,4},{5,6},{7,8},{9,10},{11,12},{13,14},{2,1},{4,3},{6,5},{... | collective-permute-start | bytes 983048 | tf_op jit(solution)/shard_map/ppermute | solution.py:354
  135.2 14.0 %collective-permute-start.28 = (bf16[4,160,256]{2,1,0:T(8,128)(2,1)S(1)}, bf16[4,160,256]{2,1,0:T(8,128)(2,1)S(1)}, u32[]{:S(2)}, u32[]{:S(2)}) collective-permute-start(bf16[4,160,256]{2,1,0:T(8,128)(2,1)S(1)} %get-tuple-element.130), channel_id=1, source_target_pairs={{1,2},{3,4},{5,6},{7,8},{9,10},{11,12},{13,14},{2,1},{4,3},{6,5},{... | collective-permute-start | bytes 983048 | tf_op jit(solution)/shard_map/ppermute | solution.py:354
  145.5 14.1 %collective-permute-start.22 = (bf16[4,160,256]{2,1,0:T(8,128)(2,1)S(1)}, bf16[4,160,256]{2,1,0:T(8,128)(2,1)S(1)}, u32[]{:S(2)}, u32[]{:S(2)}) collective-permute-start(bf16[4,160,256]{2,1,0:T(8,128)(2,1)S(1)} %get-tuple-element.115), channel_id=1, source_target_pairs={{1,2},{3,4},{5,6},{7,8},{9,10},{11,12},{13,14},{2,1},{4,3},{6,5},{... | collective-permute-start | bytes 983048 | tf_op jit(solution)/shard_map/ppermute | solution.py:354
  155.0 15.6 %collective-permute-start.30 = (bf16[4,160,256]{2,1,0:T(8,128)(2,1)S(1)}, bf16[4,160,256]{2,1,0:T(8,128)(2,1)S(1)}, u32[]{:S(2)}, u32[]{:S(2)}) collective-permute-start(bf16[4,160,256]{2,1,0:T(8,128)(2,1)S(1)} %get-tuple-element.135), channel_id=1, source_target_pairs={{1,2},{3,4},{5,6},{7,8},{9,10},{11,12},{13,14},{2,1},{4,3},{6,5},{... | collective-permute-start | bytes 983048 | tf_op jit(solution)/shard_map/ppermute | solution.py:354
  166.2 13.9 %collective-permute-start.32 = (bf16[4,160,256]{2,1,0:T(8,128)(2,1)S(1)}, bf16[4,160,256]{2,1,0:T(8,128)(2,1)S(1)}, u32[]{:S(2)}, u32[]{:S(2)}) collective-permute-start(bf16[4,160,256]{2,1,0:T(8,128)(2,1)S(1)} %get-tuple-element.139), channel_id=1, source_target_pairs={{1,2},{3,4},{5,6},{7,8},{9,10},{11,12},{13,14},{2,1},{4,3},{6,5},{... | collective-permute-start | bytes 983048 | tf_op jit(solution)/shard_map/ppermute | solution.py:354
  187.0 13.4 %collective-permute-start.34 = (f32[8,64,256]{2,1,0:T(8,128)S(1)}, f32[8,64,256]{2,1,0:T(8,128)S(1)}, u32[]{:S(2)}, u32[]{:S(2)}) collective-permute-start(f32[8,64,256]{2,1,0:T(8,128)S(1)} %get-tuple-element.144), channel_id=1, source_target_pairs={{0,16},{1,49},{2,18},{3,51},{4,20},{5,53},{6,22},{7,55},{8,24},{9,... | collective-permute-start | bytes 1572872 | tf_op jit(solution)/shard_map/ppermute | solution.py:363
  189.5 15.2 %collective-permute-start.33 = (f32[8,64,256]{2,1,0:T(8,128)S(1)}, f32[8,64,256]{2,1,0:T(8,128)S(1)}, u32[]{:S(2)}, u32[]{:S(2)}) collective-permute-start(f32[8,64,256]{2,1,0:T(8,128)S(1)} %get-tuple-element.143), channel_id=1, source_target_pairs={{0,16},{16,32},{32,48},{48,0},{64,80},{80,96},{96,112},{112,64},{1... | collective-permute-start | bytes 1572872 | tf_op jit(solution)/shard_map/ppermute | solution.py:364
  189.5 16.5 %collective-permute-start.36 = (f32[8,64,256]{2,1,0:T(8,128)S(1)}, f32[8,64,256]{2,1,0:T(8,128)S(1)}, u32[]{:S(2)}, u32[]{:S(2)}) collective-permute-start(f32[8,64,256]{2,1,0:T(8,128)S(1)} %get-tuple-element.145), channel_id=1, source_target_pairs={{0,48},{16,0},{32,16},{48,32},{64,112},{80,64},{96,80},{112,96},{1... | collective-permute-start | bytes 1572872 | tf_op jit(solution)/shard_map/ppermute | solution.py:364
  212.2 13.8 %collective-permute-start.37 = (f32[8,64,256]{2,1,0:T(8,128)S(1)}, f32[8,64,256]{2,1,0:T(8,128)S(1)}, u32[]{:S(2)}, u32[]{:S(2)}) collective-permute-start(f32[8,64,256]{2,1,0:T(8,128)S(1)} %get-tuple-element.147), channel_id=1, source_target_pairs={{0,64},{16,80},{32,96},{48,112},{64,0},{80,16},{96,32},{112,48},{1... | collective-permute-start | bytes 1572872 | tf_op jit(solution)/shard_map/ppermute | solution.py:445
  (34 other events, 247.8 us)
